TPU v7x, 32 devices: a whole 2x2x4 slice. The times are simulated.
32 devices in a mesh: grp: 8 (over z, x), row: 4 (over y, core).
Axes of the slice: x: 2, y: 2, z: 4, core: 2. Of those that a mesh axis runs over, the one named last changes fastest.
Arguments:
- item_owner: int32 [32, 1024, 1], P(('grp', 'row')), may hold values from 0 to 3; in each aligned block of 1024 rows (0 to 1023, 1024 to 2047, ..., all dimensions but the last counted through in order) at most 512 rows name the same one
- item_row: int32 [32, 1024], P(('grp', 'row')), may hold values from 0 to 50047
- seg: int32 [32, 1024], P(('grp', 'row')), may hold values from 0 to 7, never falling along the last dimension, each value on 1 to 512 neighbouring positions
- query_slot: int32 [32, 256], P(('grp', 'row')), may hold values from 0 to 1023, as said below
- tgt_owner: int32 [32, 256, 1], P(('grp', 'row')), may hold values from 0 to 3; in each aligned block of 256 rows (0 to 255, 256 to 511, ..., all dimensions but the last counted through in order) at most 128 rows name the same one
- tgt_row: int32 [32, 256], P(('grp', 'row')), may hold values from 0 to 50047
- freq_idx: int32 [32, 256], P(('grp', 'row')), may hold values from 0 to 1023
- valid: int32 [32, 256], P(('grp', 'row')), may hold values from 0 to 1
- logfreq: bfloat16 [1024], replicated, may hold values from -3 to 0
- table_w: float32 [200192, 256], P(('row', 'grp')), may hold values from -6 to 6
- table_m: float32 [200192, 256], P(('row', 'grp')), may hold values from -0.00048828125 to 0.00048828125
- table_a: float32 [200192, 256], P(('row', 'grp')), may hold values from -6 to 6
- attn_w: float32 [256, 1024], P(('grp', 'row')), may hold values from -0.375 to 0.375
- attn_m: float32 [256, 1024], P(('grp', 'row')), may hold values from -0.0390625 to 0.0390625
- attn_a: float32 [256, 1024], P(('grp', 'row')), may hold values from -0.375 to 0.375
- ffn_w: float32 [256, 2048], P(('grp', 'row')), may hold values from -0.375 to 0.375
- ffn_m: float32 [256, 2048], P(('grp', 'row')), may hold values from -0.0390625 to 0.0390625
- ffn_a: float32 [256, 2048], P(('grp', 'row')), may hold values from -0.375 to 0.375
- pos_w: float32 [256, 512], P(('grp', 'row')), may hold values from -6 to 6
- pos_m: float32 [256, 512], P(('grp', 'row')), may hold values from -0.0390625 to 0.0390625
- pos_a: float32 [256, 512], P(('grp', 'row')), may hold values from -6 to 6
- small_w: float32 [256, 11], P(('grp', 'row'))
- small_m: float32 [256, 11], P(('grp', 'row')), may hold values from -0.0390625 to 0.0390625
- small_a: float32 [256, 11], P(('grp', 'row'))
Outputs:
- loss: float32 [], replicated
- table_w_new: float32 [200192, 256], P(('row', 'grp'))
- table_m_new: float32 [200192, 256], P(('row', 'grp'))
- table_a_new: float32 [200192, 256], P(('row', 'grp'))
- table_copy: bfloat16 [200192, 256], P(('row', 'grp'))
- attn_w_new: float32 [256, 1024], P(('grp', 'row'))
- attn_m_new: float32 [256, 1024], P(('grp', 'row'))
- attn_a_new: float32 [256, 1024], P(('grp', 'row'))
- attn_copy: bfloat16 [256, 1024], P(('grp', 'row'))
- ffn_w_new: float32 [256, 2048], P(('grp', 'row'))
- ffn_m_new: float32 [256, 2048], P(('grp', 'row'))
- ffn_a_new: float32 [256, 2048], P(('grp', 'row'))
- ffn_copy: bfloat16 [256, 2048], P(('grp', 'row'))
- pos_w_new: float32 [256, 512], P(('grp', 'row'))
- pos_m_new: float32 [256, 512], P(('grp', 'row'))
- pos_a_new: float32 [256, 512], P(('grp', 'row'))
- pos_copy: bfloat16 [256, 512], P(('grp', 'row'))
- small_w_new: float32 [256, 11], P(('grp', 'row'))
- small_m_new: float32 [256, 11], P(('grp', 'row'))
- small_a_new: float32 [256, 11], P(('grp', 'row'))
- small_copy: bfloat16 [256, 11], P(('grp', 'row'))
Inputs may be any that keep to these rules, and one draw needn't show every extreme that they name: `item_owner`: in each packed row no table shard is named by more than 512 slots, and in some rows one shard by exactly 512. `seg`: history numbers of a packed row start at 0 and never fall; a history has 1 to 512 slots. `query_slot`: the 256 slots of a packed row are distinct and rising. `tgt_owner`: in each packed row no table shard is named by more than 128 targets, and in some rows one shard by exactly 128.
All inputs are finite; a program needn't handle non-finite values.
Results may differ from a plain program's by a relative error of at most 0.0085.
The roundings to bfloat16 on the way count: a program that leaves them out, or rounds other values in their place, can miss the bound.
Values may be sent and summed in bfloat16 or wider, within the bound.
No kernel may reach another device: no remote copies, remote signals or barrier semaphores. Data moves between devices by JAX's collectives and lax.ppermute only.
A program may use at most 256 MiB of HBM per device.

v0:
```python
import math

import jax
import jax.numpy as jnp
from jax import lax
from jax.sharding import PartitionSpec as P

D = 256
HEADS = 8
HEAD = 32
FF = 1024


norm_eps = 1e-05
score_scale = 0.125
logit_scale = 0.125
momentum_rate = 0.5
average_rate = 0.5
highest = lax.Precision.HIGHEST
negative = -1e30


def normed(values, gain, shift):
    centre = values - jnp.mean(values, axis=-1, keepdims=True)
    spread = jnp.mean(centre * centre, axis=-1, keepdims=True)
    return centre * lax.rsqrt(spread + norm_eps) * gain + shift


def positions(seg_row):
    slot_index = jnp.arange(seg_row.shape[0], dtype=jnp.int32)
    before = jnp.sum((seg_row[None, :] < seg_row[:, None]).astype(jnp.int32), axis=1)
    return (slot_index - before, slot_index)


def bucket_places(owner_ids, owners, offset, width):
    onehot = (owner_ids[:, None] == jnp.arange(owners, dtype=jnp.int32)[None, :]).astype(jnp.int32)
    earlier = jnp.sum((jnp.cumsum(onehot, axis=0) - onehot) * onehot, axis=1)
    return owner_ids * width + offset + earlier


def masked_scores(rows_q, heads_k, start, seg_row):
    length = rows_q.shape[0]
    slot_index = jnp.arange(seg_row.shape[0], dtype=jnp.int32)
    rows_index = start + jnp.arange(length, dtype=jnp.int32)
    rows_seg = lax.dynamic_slice_in_dim(seg_row, start, length, 0)
    scores = (
        jnp.einsum("qhd,khd->hqk", rows_q, heads_k, preferred_element_type=jnp.float32)
        * score_scale
    )
    allowed = (rows_seg[:, None] == seg_row[None, :]) & (rows_index[:, None] >= slot_index[None, :])
    return jnp.where(allowed[None], scores, negative)


def attention(heads_q, heads_k, heads_v, seg_row):
    slots = heads_q.shape[0]
    rows_block = min(512, slots)

    def one_block(step):
        start = step * rows_block
        rows_q = lax.dynamic_slice_in_dim(heads_q, start, rows_block, 0)
        scores = masked_scores(rows_q, heads_k, start, seg_row)
        row_top = jnp.max(scores, axis=2, keepdims=True)
        log_total = row_top + jnp.log(jnp.sum(jnp.exp(scores - row_top), axis=2, keepdims=True))
        probs = jnp.exp(scores - log_total).astype(jnp.bfloat16)
        mixed = jnp.einsum("hqk,khd->qhd", probs, heads_v, preferred_element_type=jnp.float32)
        return (mixed, log_total)

    mixed, log_total = lax.map(one_block, jnp.arange(slots // rows_block, dtype=jnp.int32))
    return (mixed.reshape(heads_q.shape), log_total)


def attention_back(heads_q, heads_k, heads_v, grad_out, log_total, seg_row):
    slots = heads_q.shape[0]
    rows_block = min(512, slots)

    def one_block(carry, step):
        grad_k, grad_v = carry
        start = step * rows_block
        rows_q = lax.dynamic_slice_in_dim(heads_q, start, rows_block, 0)
        rows_grad = lax.dynamic_slice_in_dim(grad_out, start, rows_block, 0)
        probs = jnp.exp(masked_scores(rows_q, heads_k, start, seg_row) - log_total[step])
        grad_p = jnp.einsum("qhd,khd->hqk", rows_grad, heads_v, preferred_element_type=jnp.float32)
        inner = jnp.sum(probs * grad_p, axis=2, keepdims=True)
        grad_s = (probs * (grad_p - inner)).astype(jnp.bfloat16)
        grad_q = (
            jnp.einsum("hqk,khd->qhd", grad_s, heads_k, preferred_element_type=jnp.float32)
            * score_scale
        )
        grad_k = (
            grad_k
            + jnp.einsum("hqk,qhd->khd", grad_s, rows_q, preferred_element_type=jnp.float32)
            * score_scale
        )
        grad_v = grad_v + jnp.einsum(
            "hqk,qhd->khd",
            probs.astype(jnp.bfloat16),
            rows_grad,
            preferred_element_type=jnp.float32,
        )
        return ((grad_k, grad_v), grad_q)

    zeros_kv = jnp.zeros(heads_k.shape, jnp.float32)
    (grad_k, grad_v), grad_q = lax.scan(
        one_block, (zeros_kv, zeros_kv), jnp.arange(slots // rows_block, dtype=jnp.int32)
    )
    return (grad_q.reshape(heads_q.shape), grad_k, grad_v)


def contract_rows(left, right):
    return lax.dot_general(
        left, right, (((0,), (0,)), ((), ())), preferred_element_type=jnp.float32
    )


def contract_cols(left, right):
    return lax.dot_general(
        left, right, (((1,), (1,)), ((), ())), preferred_element_type=jnp.float32
    )


def layer_forward(first, seg_row, attn, ffn, small):
    slots = first.shape[0]
    gain_cols = small.astype(jnp.float32)
    normed_a = normed(first, gain_cols[:, 0], gain_cols[:, 1]).astype(jnp.bfloat16)
    joined = jnp.dot(normed_a, attn[:, : 3 * D], preferred_element_type=jnp.float32).astype(
        jnp.bfloat16
    )
    heads_q = joined[:, :D].reshape(slots, HEADS, HEAD)
    heads_k = joined[:, D : 2 * D].reshape(slots, HEADS, HEAD)
    heads_v = joined[:, 2 * D :].reshape(slots, HEADS, HEAD)
    mixed, log_total = attention(heads_q, heads_k, heads_v, seg_row)
    mixed = mixed.reshape(slots, D).astype(jnp.bfloat16)
    second = first + jnp.dot(mixed, attn[:, 3 * D :], preferred_element_type=jnp.float32)
    normed_b = normed(second, gain_cols[:, 2], gain_cols[:, 3]).astype(jnp.bfloat16)
    hidden = jnp.dot(normed_b, ffn[:, :FF], preferred_element_type=jnp.float32) + gain_cols[
        :, 7:
    ].T.reshape(FF)
    active = jax.nn.relu(hidden).astype(jnp.bfloat16)
    third = second + contract_cols(active, ffn[:, FF:]) + gain_cols[:, 6]
    kept = (
        first,
        second,
        normed_a,
        heads_q,
        heads_k,
        heads_v,
        log_total,
        mixed,
        normed_b,
        hidden,
        active,
    )
    return (third, kept)


def layer_backward(grad_third, kept, seg_row, attn, ffn, small):
    (
        first,
        second,
        normed_a,
        heads_q,
        heads_k,
        heads_v,
        log_total,
        mixed,
        normed_b,
        hidden,
        active,
    ) = kept
    slots = first.shape[0]
    gain_cols = small.astype(jnp.float32)
    grad_f = grad_third.astype(jnp.bfloat16)
    grad_down = contract_rows(grad_f, active)
    grad_active = jnp.dot(grad_f, ffn[:, FF:], preferred_element_type=jnp.float32)
    grad_hidden = jnp.where(hidden > 0, grad_active, 0.0).astype(jnp.bfloat16)
    grad_up = contract_rows(normed_b, grad_hidden)
    grad_b = contract_cols(grad_hidden, ffn[:, :FF])
    norm_back = jax.vjp(normed, second, gain_cols[:, 2], gain_cols[:, 3])[1](grad_b)
    grad_second = grad_third + norm_back[0]
    grad_y = grad_second.astype(jnp.bfloat16)
    grad_proj = contract_rows(mixed, grad_y)
    grad_mixed = (
        contract_cols(grad_y, attn[:, 3 * D :]).astype(jnp.bfloat16).reshape(slots, HEADS, HEAD)
    )
    grad_q, grad_k, grad_v = attention_back(
        heads_q, heads_k, heads_v, grad_mixed, log_total, seg_row
    )
    grad_joined = jnp.concatenate(
        [grad_q.reshape(slots, D), grad_k.reshape(slots, D), grad_v.reshape(slots, D)], axis=1
    ).astype(jnp.bfloat16)
    grad_qkv = contract_rows(normed_a, grad_joined)
    grad_a = contract_cols(grad_joined, attn[:, : 3 * D])
    first_back = jax.vjp(normed, first, gain_cols[:, 0], gain_cols[:, 1])[1](grad_a)
    grad_first = grad_second + first_back[0]
    grad_attn = jnp.concatenate([grad_qkv, grad_proj], axis=1)
    grad_ffn = jnp.concatenate([grad_up, grad_down], axis=1)
    columns = (
        first_back[1],
        first_back[2],
        norm_back[1],
        norm_back[2],
        jnp.sum(grad_f.astype(jnp.float32), axis=0),
        jnp.sum(grad_hidden.astype(jnp.float32), axis=0),
    )
    return (grad_first, grad_attn, grad_ffn, columns)


def advance(weight, moment, average, grad, rate):
    moment_new = momentum_rate * moment + grad
    weight_new = weight - rate * (grad + momentum_rate * moment_new)
    average_new = average_rate * average + (1.0 - average_rate) * weight_new
    return (weight_new, moment_new, average_new, weight_new.astype(jnp.bfloat16))


def local(
    item_owner,
    item_row,
    seg,
    query_slot,
    tgt_owner,
    tgt_row,
    freq_idx,
    valid,
    logfreq,
    table_w,
    table_m,
    table_a,
    attn_w,
    attn_m,
    attn_a,
    ffn_w,
    ffn_m,
    ffn_a,
    pos_w,
    pos_m,
    pos_a,
    small_w,
    small_m,
    small_a,
):
    owners = lax.axis_size("row")
    devices = lax.axis_size("grp") * owners
    shard_rows = table_w.shape[0] * lax.axis_size("grp")
    slots = seg.shape[1]
    queries = query_slot.shape[1]
    cap_items = 2 * slots // owners
    cap_targets = 2 * queries // owners
    width = cap_items + cap_targets
    total_q = queries * devices
    attn, ffn, pos, small = (
        lax.all_gather(attn_w.astype(jnp.bfloat16), ("grp", "row"), axis=0, tiled=True),
        lax.all_gather(ffn_w.astype(jnp.bfloat16), ("grp", "row"), axis=0, tiled=True),
        lax.all_gather(pos_w.astype(jnp.bfloat16), ("grp", "row"), axis=0, tiled=True),
        lax.all_gather(small_w.astype(jnp.bfloat16), ("grp", "row"), axis=0, tiled=True),
    )
    table = lax.all_gather(table_w.astype(jnp.bfloat16), "grp", axis=0, tiled=True)
    item_places = bucket_places(item_owner[0, :, 0], owners, 0, width)
    target_places = bucket_places(tgt_owner[0, :, 0], owners, cap_items, width)
    all_places = jnp.concatenate([item_places, target_places])
    wanted = (
        jnp.full((owners * width,), -1, jnp.int32)
        .at[all_places]
        .set(jnp.concatenate([item_row[0], tgt_row[0]]))
    )
    asked = lax.all_to_all(
        wanted.reshape(owners, width), "row", split_axis=0, concat_axis=0, tiled=True
    )
    rows_found = jnp.where(
        (asked >= 0)[..., None], table[jnp.maximum(asked, 0)], jnp.zeros((), jnp.bfloat16)
    )
    found, asked = (
        lax.all_to_all(rows_found, "row", split_axis=0, concat_axis=0, tiled=True),
        asked,
    )
    found = found.reshape(owners * width, D)
    item_emb = found[item_places]
    target_emb = found[target_places]
    seg_row = seg[0]
    places, slot_index = positions(seg_row)
    pos_hot = (places[:, None] == jnp.arange(pos.shape[1], dtype=jnp.int32)[None, :]).astype(
        jnp.bfloat16
    )
    first = item_emb.astype(jnp.float32) + contract_cols(pos_hot, pos)
    third, kept = layer_forward(first, seg_row, attn, ffn, small)
    gain_cols = small.astype(jnp.float32)
    final, final_back = jax.vjp(normed, third, gain_cols[:, 4], gain_cols[:, 5])
    slots_q = query_slot[0]
    query_h = final[slots_q].astype(jnp.bfloat16)
    freq_hot = (
        freq_idx[0][:, None] == jnp.arange(logfreq.shape[0], dtype=jnp.int32)[None, :]
    ).astype(jnp.bfloat16)
    corr_own = jnp.dot(freq_hot, logfreq, preferred_element_type=jnp.float32).astype(jnp.bfloat16)
    flags = valid[0]
    valid_total = lax.psum(jnp.sum(flags).astype(jnp.float32), ("grp", "row"))
    target_all, corr_all = (
        lax.all_gather(target_emb, ("grp", "row"), axis=0, tiled=True),
        lax.all_gather(corr_own, ("grp", "row"), axis=0, tiled=True),
    )
    valid_total = jnp.maximum(valid_total, 1.0)
    weight = flags.astype(jnp.float32) / valid_total
    corr_all = corr_all.astype(jnp.float32)
    cols_block = queries * min(devices, 16)
    blocks_count = total_q // cols_block
    device_rank = lax.axis_index("grp") * owners + lax.axis_index("row")
    own_cols = device_rank * queries + jnp.arange(queries, dtype=jnp.int32)

    def logits_of(start, width_cols):
        cols = lax.dynamic_slice_in_dim(target_all, start, width_cols, 0)
        shift = lax.dynamic_slice_in_dim(corr_all, start, width_cols, 0)
        return (contract_cols(query_h, cols) * logit_scale - shift[None, :], cols)

    def scan_totals(carry, step):
        row_top, row_total = carry
        logits, unused = logits_of(step * cols_block, cols_block)
        new_top = jnp.maximum(row_top, jnp.max(logits, axis=1))
        row_total = row_total * jnp.exp(row_top - new_top) + jnp.sum(
            jnp.exp(logits - new_top[:, None]), axis=1
        )
        return ((new_top, row_total), None)

    start_top = jnp.full((queries,), negative, jnp.float32)
    (row_top, row_total), unused = lax.scan(
        scan_totals,
        (start_top, jnp.zeros((queries,), jnp.float32)),
        jnp.arange(blocks_count, dtype=jnp.int32),
    )
    log_total = row_top + jnp.log(row_total)
    own = jnp.sum(
        query_h.astype(jnp.float32) * target_emb.astype(jnp.float32), axis=1
    ) * logit_scale - corr_own.astype(jnp.float32)
    loss_local = jnp.sum(weight * (log_total - own))

    def coefficients(logits, start, width_cols):
        cols_index = start + jnp.arange(width_cols, dtype=jnp.int32)
        hit = (own_cols[:, None] == cols_index[None, :]).astype(jnp.float32)
        return (weight[:, None] * (jnp.exp(logits - log_total[:, None]) - hit)).astype(jnp.bfloat16)

    def query_grads(acc, step):
        logits, cols = logits_of(step * cols_block, cols_block)
        coeff = coefficients(logits, step * cols_block, cols_block)
        return (acc + jnp.dot(coeff, cols, preferred_element_type=jnp.float32), None)

    grad_query, unused = lax.scan(
        query_grads, jnp.zeros((queries, D), jnp.float32), jnp.arange(blocks_count, dtype=jnp.int32)
    )
    grad_query = grad_query * logit_scale
    piece = math.gcd(queries * lax.axis_size(("grp", "row")), cols_block)

    def one_piece(step):
        begin = step * piece
        logits, unused_cols = logits_of(begin, piece)
        return contract_rows(coefficients(logits, begin, piece), query_h) * logit_scale

    grad_target = lax.psum_scatter(
        lax.map(
            one_piece, jnp.arange(queries * lax.axis_size(("grp", "row")) // piece, dtype=jnp.int32)
        ).reshape(queries * lax.axis_size(("grp", "row")), D),
        ("grp", "row"),
        scatter_dimension=0,
        tiled=True,
    )
    grad_final = jnp.zeros((slots, D), jnp.float32).at[slots_q].add(grad_query)
    grad_third, grad_gain_f, grad_shift_f = final_back(grad_final)
    grad_first, grad_attn, grad_ffn, columns = layer_backward(
        grad_third, kept, seg_row, attn, ffn, small
    )
    grad_pos = lax.dot_general(
        grad_first,
        pos_hot.astype(jnp.float32),
        (((0,), (0,)), ((), ())),
        precision=highest,
        preferred_element_type=jnp.float32,
    )
    bias_cols = columns[5].reshape(FF // D, D).T
    grad_small = jnp.concatenate(
        [
            jnp.stack(
                [
                    columns[0],
                    columns[1],
                    columns[2],
                    columns[3],
                    grad_gain_f,
                    grad_shift_f,
                    columns[4],
                ],
                axis=1,
            ),
            bias_cols,
        ],
        axis=1,
    )
    sent = (
        jnp.zeros((owners * width, D), jnp.float32)
        .at[item_places]
        .set(grad_first)
        .at[target_places]
        .set(grad_target)
    )
    received = lax.all_to_all(
        sent.reshape(owners, width, D).astype(jnp.bfloat16),
        "row",
        split_axis=0,
        concat_axis=0,
        tiled=True,
    ).astype(jnp.float32)
    live = (asked >= 0)[..., None]
    partial_rows = (
        jnp.zeros((shard_rows, D), jnp.float32)
        .at[jnp.maximum(asked, 0).reshape(-1)]
        .add(jnp.where(live, received, 0.0).reshape(-1, D))
    )
    grad_table = lax.psum_scatter(
        partial_rows.astype(jnp.bfloat16), "grp", scatter_dimension=0, tiled=True
    ).astype(jnp.float32)
    grad_attn, grad_ffn, grad_pos, grad_small = (
        lax.psum_scatter(grad_attn, ("grp", "row"), scatter_dimension=0, tiled=True),
        lax.psum_scatter(grad_ffn, ("grp", "row"), scatter_dimension=0, tiled=True),
        lax.psum_scatter(grad_pos, ("grp", "row"), scatter_dimension=0, tiled=True),
        lax.psum_scatter(grad_small, ("grp", "row"), scatter_dimension=0, tiled=True),
    )
    loss = lax.psum(loss_local, ("grp", "row"))
    rate_table = 4.0 * total_q
    rate_dense = 0.25 * math.sqrt(total_q)
    rate_place = 2.0 * math.sqrt(total_q)
    return (
        (loss,)
        + advance(table_w, table_m, table_a, grad_table, rate_table)
        + advance(attn_w, attn_m, attn_a, grad_attn, rate_dense)
        + advance(ffn_w, ffn_m, ffn_a, grad_ffn, rate_dense)
        + advance(pos_w, pos_m, pos_a, grad_pos, rate_place)
        + advance(small_w, small_m, small_a, grad_small, rate_dense)
    )


def solution(mesh):
    in_specs = (
        P(("grp", "row"), None, None),
        P(("grp", "row"), None),
        P(("grp", "row"), None),
        P(("grp", "row"), None),
        P(("grp", "row"), None, None),
        P(("grp", "row"), None),
        P(("grp", "row"), None),
        P(("grp", "row"), None),
        P(),
        P(("row", "grp"), None),
        P(("row", "grp"), None),
        P(("row", "grp"), None),
        P(("grp", "row"), None),
        P(("grp", "row"), None),
        P(("grp", "row"), None),
        P(("grp", "row"), None),
        P(("grp", "row"), None),
        P(("grp", "row"), None),
        P(("grp", "row"), None),
        P(("grp", "row"), None),
        P(("grp", "row"), None),
        P(("grp", "row"), None),
        P(("grp", "row"), None),
        P(("grp", "row"), None),
    )
    out_specs = (
        P(),
        P(("row", "grp"), None),
        P(("row", "grp"), None),
        P(("row", "grp"), None),
        P(("row", "grp"), None),
        P(("grp", "row"), None),
        P(("grp", "row"), None),
        P(("grp", "row"), None),
        P(("grp", "row"), None),
        P(("grp", "row"), None),
        P(("grp", "row"), None),
        P(("grp", "row"), None),
        P(("grp", "row"), None),
        P(("grp", "row"), None),
        P(("grp", "row"), None),
        P(("grp", "row"), None),
        P(("grp", "row"), None),
        P(("grp", "row"), None),
        P(("grp", "row"), None),
        P(("grp", "row"), None),
        P(("grp", "row"), None),
    )
    return jax.shard_map(local, mesh=mesh, in_specs=in_specs, out_specs=out_specs, check_vma=False)
```

profile of v0, /device:TPU:0, one launch (start us, length us, event | category | flops | bytes accessed | tf_op | source)
XLA Modules:
  0.0 1751.2 jit_solution(13920874241432915818)
XLA Ops:
  7.3 4.8 convert_element_type.162
  15.6 5.3 scatter_custom_fusion
  21.5 4.2 all-to-all-start
  27.7 74.9 %psum.14 = f32[]{:T(128)} all-reduce(f32[]{:T(128)S(6)} %convert_element_type.157), channel_id=1, replica_groups=mesh['grp'=8,'row'=4] {'grp','row'}, use_global_device_ids=true, to_apply=%region_1.2 | all-reduce | flops 1 | bytes 8 | tf_op jit(solution)/shard_map/psum | solution.py:294
  104.5 42.7 %all_gather.24 = bf16[256,11]{1,0:T(8,128)(2,1)S(1)} all-gather(bf16[8,11]{1,0:T(8,128)(2,1)S(1)} %convert_element_type.166), channel_id=1, replica_groups=mesh['grp'=8,'row'=4] {'grp','row'}, dimensions={0}, use_global_device_ids=true | all-gather | bytes 5808 | tf_op jit(solution)/shard_map/all_gather | solution.py:254
  148.4 357.4 %all-gather.6.cloned.1.call-done = bf16[50048,256]{1,0:T(8,128)(2,1)} async-done(((bf16[6256,256]{1,0:T(8,128)(2,1)}), bf16[50048,256]{1,0:T(8,128)(2,1)}) %all-gather.6.cloned.1.call-update) | async-done | bytes 25624592 | tf_op jit(solution)/shard_map/all_gather | solution.py:256
  505.8 17.3 gather_fusion
  524.7 3.5 all-to-all-start.1
  528.4 49.0 %all-gather.1 = bf16[32,1,256]{2,1,0:T(2,128)(2,1)S(1)} all-gather(bf16[1,1,256]{2,1,0:T(2,128)(2,1)S(1)} %reshape.674), channel_id=1, replica_groups=mesh['grp'=8,'row'=4] {'grp','row'}, dimensions={0}, use_global_device_ids=true | all-gather | bytes 16896 | tf_op jit(solution)/shard_map/all_gather | solution.py:297
  577.5 37.3 %all_gather.23 = bf16[256,512]{1,0:T(8,128)(2,1)S(1)} all-gather(bf16[8,512]{1,0:T(8,128)(2,1)S(1)} %convert_element_type.165), channel_id=1, replica_groups=mesh['grp'=8,'row'=4] {'grp','row'}, dimensions={0}, use_global_device_ids=true | all-gather | bytes 270336 | tf_op jit(solution)/shard_map/all_gather | solution.py:253
  614.9 39.6 %all_gather.25 = bf16[256,1024]{1,0:T(8,128)(2,1)S(1)} all-gather(bf16[8,1024]{1,0:T(8,128)(2,1)S(1)} %convert_element_type.169), channel_id=1, replica_groups=mesh['grp'=8,'row'=4] {'grp','row'}, dimensions={0}, use_global_device_ids=true | all-gather | bytes 540672 | tf_op jit(solution)/shard_map/all_gather | solution.py:251
  656.3 3.9 gather_fusion.2
  664.5 29.8 %while.62 = (s32[]{:T(128)}, bf16[2,512,8,32]{1,3,2,0:T(8,128)(2,1)}, f32[2,8,512,1]{2,1,3,0:T(8,128)S(1)}, s32[2]{0:T(128)S(1)}, s32[1024]{0:T(1024)S(1)}, /*in...) while((s32[]{:T(128)}, ...), condition=%wide.region_15.16_spmd, body=%wide.region_12.15_spmd.sunk | while | flops 584577536 | bytes 58603788 | solution.py:68
  666.4 3.0 fusion.203
  669.4 4.2 exponential_reduce_fusion.4
  673.7 4.8 fusion.204
  681.3 3.0 fusion.203
  684.3 4.2 exponential_reduce_fusion.4
  688.6 4.8 fusion.204
  697.5 2.4 fusion.103
  707.2 14.8 all-gather.10.cloned.1.call-done
  722.0 8.7 while.64
  723.3 2.4 fusion.210
  727.6 2.4 fusion.210
  731.3 12.3 while.65
  733.0 4.6 fusion.216
  738.9 4.6 fusion.216
  743.6 2.9 scatter_custom_fusion.1
  746.5 2.5 copy.127
  749.1 2.4 multiply_reduce_fusion.1
  751.5 2.8 fusion.138
  754.3 11.8 while.63
  755.6 4.6 fusion.208
  761.5 4.7 fusion.208
  768.3 4.0 convert_reduce_fusion
  772.2 2.3 fusion.145
  774.6 2.5 copy.128
  785.3 87.2 %while.66 = (s32[]{:T(128)}, f32[1024,8,32]{0,2,1:T(8,128)}, f32[1024,8,32]{0,2,1:T(8,128)}, bf16[2,512,8,32]{1,3,2,0:T(8,128)(2,1)}, s32[2]{0:T(128)S(1)}, /*in...) while((s32[]{:T(128)}, f32[1024,8,32]{0,2,1:T(8,128)}, ...), condition=%wide.region_36.37_spmd.clone, body=%wide.region_34.36_spmd.clone.sunk | while | flops 1382937088 | bytes 178616848 | solution.py:103
  790.0 3.5 fusion.226
  793.5 11.1 multiply_reduce_fusion.13
  804.6 9.5 multiply_convert_fusion.2
  814.1 8.6 fusion.229
  822.8 2.6 fusion.230
  825.4 2.6 fusion.228
  832.6 3.5 fusion.226
  836.1 11.1 multiply_reduce_fusion.13
  847.2 9.4 multiply_convert_fusion.2
  856.7 8.9 fusion.229
  865.6 2.6 fusion.230
  868.2 4.0 fusion.228
  890.6 2.5 fusion.130
  897.1 5.9 scatter_custom_fusion.2
  903.0 10.7 reduce-scatter.7.cloned.1.call-done
  913.7 2.8 scatter_fusion
  916.7 20.6 %all_to_all.19 = bf16[4,640,256]{2,1,0:T(8,128)(2,1)S(1)} all-to-all(bf16[4,640,256]{2,1,0:T(8,128)(2,1)S(1)} %bitcast.244), channel_id=1, replica_groups=mesh['grp'=8,'row'=4] {'row'}, dimensions={0} | all-to-all | bytes 2621440 | tf_op jit(solution)/shard_map/all_to_all | solution.py:400
  937.8 37.2 %scatter_custom_fusion.4 = f32[50048,256]{1,0:T(8,128)} fusion(s32[2560]{0:T(1024)} %copy-done.61, f32[2560,256]{1,0:T(8,128)S(1)} %bitcast.248, f32[]{:T(128)} %constant.95.clone.1), kind=kCustom, calls=%fused_computation.102 | custom fusion | flops 655360 | bytes 51249664 | tf_op jit(solution)/shard_map/scatter-add | solution.py:411
  975.0 25.8 %convert_element_type.189 = bf16[50048,256]{1,0:T(8,128)(2,1)} convert(f32[50048,256]{1,0:T(8,128)} %scatter_custom_fusion.4) | non-fusion elementwise | flops 12812288 | bytes 76873728 | tf_op jit(solution)/shard_map/convert_element_type | solution.py:414
  1002.4 37.6 %all-reduce.1 = (f32[]{:T(128)}, f32[256,11]{0,1:T(8,128)S(1)}) all-reduce(f32[]{:T(128)} %get-tuple-element.605, f32[256,11]{0,1:T(8,128)S(1)} %concatenate.49), channel_id=1, replica_groups=mesh['grp'=8,'row'=4] {'grp','row'}, use_global_device_ids=true, to_apply=%region_26.27 | all-reduce | flops 2817 | bytes 22536 | tf_op jit(solution)/shard_map/psum | solution.py:422
  1042.8 3.3 reduce-scatter.15.cloned.1.call-done
  1048.1 131.0 %reduce-scatter.11.cloned.1.call-done = f32[8,1024]{1,0:T(8,128)} async-done(((f32[256,1024]{1,0:T(8,128)}), f32[8,1024]{1,0:T(8,128)}) %reduce-scatter.11.cloned.1.call-update) | async-done | bytes 32784 | tf_op jit(solution)/shard_map/reduce_scatter | solution.py:417
  1181.2 133.6 %reduce-scatter.13.cloned.1.call-done = f32[8,2048]{1,0:T(8,128)} async-done(((f32[256,2048]{1,0:T(8,128)}), f32[8,2048]{1,0:T(8,128)}) %reduce-scatter.13.cloned.1.call-update) | async-done | bytes 65552 | tf_op jit(solution)/shard_map/reduce_scatter | solution.py:418
  1316.9 408.5 %reduce-scatter.9.cloned.1.call-done = bf16[6256,256]{1,0:T(8,128)(2,1)} async-done(((bf16[50048,256]{1,0:T(8,128)(2,1)}), bf16[6256,256]{1,0:T(8,128)(2,1)}) %reduce-scatter.9.cloned.1.call-update) | async-done | bytes 3203088 | tf_op jit(solution)/shard_map/reduce_scatter | solution.py:413
  1725.4 9.7 fusion.135
  1735.1 8.7 add_multiply_fusion
  (435 shorter events, 82.1 us)
Async XLA Ops:
  7.2 6.6 copy-start.50
  7.2 8.4 copy-start.104
  7.2 8.4 copy-start.90
  7.2 18.5 %copy-start.94 = (s32[1,256]{1,0:T(1,128)S(1)}, s32[1,256]{1,0:T(1,128)}, u32[]{:S(2)}) copy-start(s32[1,256]{1,0:T(1,128)} %param.41) | copy-start | bytes 3076
  7.2 19.8 %copy-start.37 = (f32[8,2048]{1,0:T(8,128)S(1)}, f32[8,2048]{1,0:T(8,128)}, u32[]{:S(2)}) copy-start(f32[8,2048]{1,0:T(8,128)} %param.49) | copy-start | bytes 196612
  7.3 96.5 %copy-start.101 = (s32[1,256]{1,0:T(1,128)S(1)}, s32[1,256]{1,0:T(1,128)}, u32[]{:S(2)}) copy-start(s32[1,256]{1,0:T(1,128)} %param.37) | copy-start | bytes 3076
  7.3 96.5 %copy-start.75 = (f32[8,11]{1,0:T(8,128)S(1)}, f32[8,11]{1,0:T(8,128)}, u32[]{:S(2)}) copy-start(f32[8,11]{1,0:T(8,128)} %param.55) | copy-start | bytes 1060
  7.3 96.5 %copy-start.99 = (bf16[1024]{0:T(1024)(128)(2,1)S(1)}, bf16[1024]{0:T(1024)(128)(2,1)}, u32[]{:S(2)}) copy-start(bf16[1024]{0:T(1024)(128)(2,1)} %param.42) | copy-start | bytes 6148
  7.3 96.6 %copy-start.29 = (s32[1,1024]{1,0:T(1,128)S(1)}, s32[1,1024]{1,0:T(1,128)}, u32[]{:S(2)}) copy-start(s32[1,1024]{1,0:T(1,128)} %param.36) | copy-start | bytes 12292
  7.3 498.5 %all-gather.6.cloned.1.call-start = ((), (), s32[]{:S(2)}) async-start(), calls=%async_computation.8 | async-start | bytes 28827648 | tf_op jit(solution)/shard_map/all_gather | solution.py:256
  12.2 135.1 %copy-start.105 = (s32[1,256]{1,0:T(1,128)S(1)}, s32[1,256]{1,0:T(1,128)}, u32[]{:S(2)}) copy-start(s32[1,256]{1,0:T(1,128)} %param.40) | copy-start | bytes 3076
  21.5 126.8 %all-to-all-start = ((s32[4,1,640]{2,1,0:T(1,128)}), s32[4,1,640]{2,1,0:T(1,128)S(1)}, u32[]{:S(2)}, u32[]{:S(2)}) async-start(s32[4,1,640]{2,1,0:T(1,128)} %all_to_all.12), calls=%async_computation | async-start | bytes 20480 | tf_op jit(solution)/shard_map/all_to_all | solution.py:265
  25.7 671.7 %all-gather.8.cloned.1.call-start = ((), (), s32[]{:S(2)}) async-start(), calls=%async_computation.9 | async-start | bytes 1081344 | tf_op jit(solution)/shard_map/all_gather | solution.py:252
  103.9 511.0 %copy-start.82 = (s32[256,1]{0,1:T(1,128)}, s32[256,1]{0,1:T(1,128)S(1)}, u32[]{:S(2)}) copy-start(s32[256,1]{0,1:T(1,128)S(1)} %compare_select_fusion.3) | copy-start | bytes 3076
  104.5 556.0 %copy-start.91 = (s32[1024]{0:T(1024)}, s32[1024]{0:T(1024)S(1)}, u32[]{:S(2)}) copy-start(s32[1024]{0:T(1024)S(1)} %iota_subtract_fusion) | copy-start | bytes 12292
  147.7 380.7 %copy-start.102 = (f32[1,256]{1,0:T(1,128)}, f32[1,256]{1,0:T(1,128)S(1)}, u32[]{:S(2)}) copy-start(f32[1,256]{1,0:T(1,128)S(1)} %fusion.92) | copy-start | bytes 3076
  148.2 513.7 %copy-start.70 = (f32[256]{0:T(256)}, f32[256]{0:T(256)S(1)}, u32[]{:S(2)}) copy-start(f32[256]{0:T(256)S(1)} %get-tuple-element.487) | copy-start | bytes 3076
  148.2 513.7 %copy-start.86 = (f32[256]{0:T(256)}, f32[256]{0:T(256)S(1)}, u32[]{:S(2)}) copy-start(f32[256]{0:T(256)S(1)} %get-tuple-element.486) | copy-start | bytes 3076
  148.2 549.2 %copy-start.97 = (f32[256]{0:T(256)}, f32[256]{0:T(256)S(1)}, u32[]{:S(2)}) copy-start(f32[256]{0:T(256)S(1)} %get-tuple-element.484) | copy-start | bytes 3076
  148.2 630.9 %copy-start.80 = (f32[256]{0:T(256)}, f32[256]{0:T(256)S(1)}, u32[]{:S(2)}) copy-start(f32[256]{0:T(256)S(1)} %get-tuple-element.485) | copy-start | bytes 3076
  148.3 374.8 %copy-start.72 = (pred[4,1,640]{2,0,1:T(4,128)(4,1)}, pred[4,1,640]{2,0,1:T(4,128)(4,1)S(1)}, u32[]{:S(2)}) copy-start(pred[4,1,640]{2,0,1:T(4,128)(4,1)S(1)} %copy.155) | copy-start | bytes 7684
  148.4 357.4 %copy-start.61 = (s32[2560]{0:T(1024)}, s32[2560]{0:T(1024)S(1)}, u32[]{:S(2)}) copy-start(s32[2560]{0:T(1024)S(1)} %reshape.600) | copy-start | bytes 30724
  523.1 5.3 copy-start.45
  524.7 129.9 %all-to-all-start.1 = ((bf16[4,640,256]{2,1,0:T(8,128)(2,1)}), bf16[4,640,256]{2,1,0:T(8,128)(2,1)S(1)}, u32[]{:S(2)}, u32[]{:S(2)}) async-start(bf16[4,640,256]{2,1,0:T(8,128)(2,1)} %broadcast_select_fusion.1), calls=%async_computation.1 | async-start | bytes 2621440 | tf_op jit(solution)/shard_map/all_to_all | solution.py:272
  528.2 193.8 %all-gather.10.cloned.1.call-start = ((), (), s32[]{:S(2)}) async-start(), calls=%async_computation.15 | async-start | bytes 4325376 | tf_op jit(solution)/shard_map/all_gather | solution.py:296
  577.5 190.8 %copy-start.64 = (f32[1,2,4,128]{3,1,2,0:T(2,128)}, f32[1,2,4,128]{3,1,2,0:T(2,128)S(1)}, u32[]{:S(2)}) copy-start(f32[1,2,4,128]{3,1,2,0:T(2,128)S(1)} %copy.150) | copy-start | bytes 12292
  614.8 46.9 %copy-start.77 = (s32[1024,1]{0,1:T(1,128)}, s32[1024,1]{0,1:T(1,128)S(1)}, u32[]{:S(2)}) copy-start(s32[1024,1]{0,1:T(1,128)S(1)} %compare_select_fusion.1) | copy-start | bytes 12292
  654.5 128.7 %copy-start.21 = (bf16[256,1024]{1,0:T(8,128)(2,1)}, bf16[256,1024]{1,0:T(8,128)(2,1)S(1)}, u32[]{:S(2)}) copy-start(bf16[256,1024]{1,0:T(8,128)(2,1)S(1)} %all_gather.25) | copy-start | bytes 1572868
  661.7 34.2 %copy-start.5 = (f32[1024,256]{0,1:T(8,128)}, f32[1024,256]{0,1:T(8,128)S(1)}, u32[]{:S(2)}) copy-start(f32[1024,256]{0,1:T(8,128)S(1)} %get-tuple-element.617) | copy-start | bytes 3145732
  663.6 250.2 %reduce-scatter.7.cloned.1.call-start = ((), (), s32[]{:S(2)}) async-start(), calls=%async_computation.10 | async-start | bytes 8650752 | tf_op jit(solution)/shard_map/reduce_scatter | solution.py:354
  696.3 82.9 %copy-start.47 = (f32[1024]{0:T(1024)}, f32[1024]{0:T(1024)S(1)}, u32[]{:S(2)}) copy-start(f32[1024]{0:T(1024)S(1)} %broadcast_multiply_fusion.1) | copy-start | bytes 12292
  697.4 81.8 %copy-start.57 = (f32[1024]{0:T(1024)}, f32[1024]{0:T(1024)S(1)}, u32[]{:S(2)}) copy-start(f32[1024]{0:T(1024)S(1)} %fusion.123) | copy-start | bytes 12292
  722.0 8.7 copy-start.95
  722.0 8.7 copy-start.103
  722.0 9.3 copy-start.39
  754.3 26.5 %copy-start.59 = (f32[1024]{0:T(1024)}, f32[1024]{0:T(1024)S(1)}, u32[]{:S(2)}) copy-start(f32[1024]{0:T(1024)S(1)} %negate_multiply_fusion.2) | copy-start | bytes 12292
  766.2 280.0 %reduce-scatter.15.cloned.1.call-start = ((), (), s32[]{:S(2)}) async-start(), calls=%async_computation.14 | async-start | bytes 540672 | tf_op jit(solution)/shard_map/reduce_scatter | solution.py:419
  766.2 6.0 copy-start.32
  768.3 6.3 copy-start.23
  804.6 9.5 copy-start.12
  814.1 8.6 copy-start
  814.1 8.6 copy-start.25
  847.2 9.4 copy-start.12
  856.7 8.9 copy-start
  856.7 8.9 copy-start.25
  881.8 5.3 copy-start.87
  885.5 293.7 %reduce-scatter.11.cloned.1.call-start = ((), (), s32[]{:S(2)}) async-start(), calls=%async_computation.12 | async-start | bytes 1081344 | tf_op jit(solution)/shard_map/reduce_scatter | solution.py:417
  890.5 424.3 %reduce-scatter.13.cloned.1.call-start = ((), (), s32[]{:S(2)}) async-start(), calls=%async_computation.13 | async-start | bytes 2162688 | tf_op jit(solution)/shard_map/reduce_scatter | solution.py:418
  895.6 18.1 %copy-start.83 = (s32[256,1]{0,1:T(1,128)S(1)}, s32[256,1]{0,1:T(1,128)}, u32[]{:S(2)}) copy-start(s32[256,1]{0,1:T(1,128)} %copy-done.82) | copy-start | bytes 3076
  895.7 829.8 %reduce-scatter.9.cloned.1.call-start = ((), (), s32[]{:S(2)}) async-start(), calls=%async_computation.11 | async-start | bytes 28827648 | tf_op jit(solution)/shard_map/reduce_scatter | solution.py:413
  916.5 20.7 %copy-start.73 = (pred[4,1,640]{2,0,1:T(4,128)(4,1)S(1)}, pred[4,1,640]{2,0,1:T(4,128)(4,1)}, u32[]{:S(2)}) copy-start(pred[4,1,640]{2,0,1:T(4,128)(4,1)} %copy-done.72) | copy-start | bytes 7684
  1000.9 45.3 %copy-start.53 = (f32[8,512]{1,0:T(8,128)S(1)}, f32[8,512]{1,0:T(8,128)}, u32[]{:S(2)}) copy-start(f32[8,512]{1,0:T(8,128)} %param.52) | copy-start | bytes 49156
  1000.9 45.3 %copy-start.79 = (f32[8,512]{1,0:T(8,128)S(1)}, f32[8,512]{1,0:T(8,128)}, u32[]{:S(2)}) copy-start(f32[8,512]{1,0:T(8,128)} %param.53) | copy-start | bytes 49156
  1000.9 46.6 %copy-start.74 = (f32[8,512]{1,0:T(8,128)S(1)}, f32[8,512]{1,0:T(8,128)}, u32[]{:S(2)}) copy-start(f32[8,512]{1,0:T(8,128)} %param.54) | copy-start | bytes 49156
  1000.9 178.2 %copy-start.46 = (f32[8,1024]{1,0:T(8,128)S(1)}, f32[8,1024]{1,0:T(8,128)}, u32[]{:S(2)}) copy-start(f32[8,1024]{1,0:T(8,128)} %param.46) | copy-start | bytes 98308
  1001.0 178.2 %copy-start.69 = (f32[8,1024]{1,0:T(8,128)S(1)}, f32[8,1024]{1,0:T(8,128)}, u32[]{:S(2)}) copy-start(f32[8,1024]{1,0:T(8,128)} %param.47) | copy-start | bytes 98308
  1001.0 179.6 %copy-start.68 = (f32[8,1024]{1,0:T(8,128)S(1)}, f32[8,1024]{1,0:T(8,128)}, u32[]{:S(2)}) copy-start(f32[8,1024]{1,0:T(8,128)} %param.48) | copy-start | bytes 98308
  1001.0 313.8 %copy-start.38 = (f32[8,2048]{1,0:T(8,128)S(1)}, f32[8,2048]{1,0:T(8,128)}, u32[]{:S(2)}) copy-start(f32[8,2048]{1,0:T(8,128)} %param.49) | copy-start | bytes 196612
  1001.0 313.8 %copy-start.54 = (f32[8,2048]{1,0:T(8,128)S(1)}, f32[8,2048]{1,0:T(8,128)}, u32[]{:S(2)}) copy-start(f32[8,2048]{1,0:T(8,128)} %param.50) | copy-start | bytes 196612
  1001.0 315.3 %copy-start.49 = (f32[8,2048]{1,0:T(8,128)S(1)}, f32[8,2048]{1,0:T(8,128)}, u32[]{:S(2)}) copy-start(f32[8,2048]{1,0:T(8,128)} %param.51) | copy-start | bytes 196612
  1047.5 687.6 %copy-start.51 = (f32[8,512]{1,0:T(8,128)}, f32[8,512]{1,0:T(8,128)S(1)}, u32[]{:S(2)}) copy-start(f32[8,512]{1,0:T(8,128)S(1)} %get-tuple-element.588) | copy-start | bytes 49156
  1180.6 554.5 %copy-start.44 = (f32[8,1024]{1,0:T(8,128)}, f32[8,1024]{1,0:T(8,128)S(1)}, u32[]{:S(2)}) copy-start(f32[8,1024]{1,0:T(8,128)S(1)} %get-tuple-element.594) | copy-start | bytes 98308
  1316.3 418.8 %copy-start.36 = (f32[8,2048]{1,0:T(8,128)}, f32[8,2048]{1,0:T(8,128)S(1)}, u32[]{:S(2)}) copy-start(f32[8,2048]{1,0:T(8,128)S(1)} %get-tuple-element.591) | copy-start | bytes 196612
  1735.1 8.7 copy-start.11
  (63 other events, 178.2 us)
Sparse Core Ops, SparseCore 0:
  12.3 493.4 all-gather.5
  509.2 53.7 all-gather.7
  663.7 58.2 all-gather.9
  766.3 147.3 reduce-scatter.6
  915.8 130.3 reduce-scatter.14
  1048.4 130.7 reduce-scatter.10
  1182.0 132.7 reduce-scatter.12
  1318.9 406.4 reduce-scatter.8
where the time goes:
time: 1760 us; the launch traced here: 1750 us
  waiting for transfers between devices  1060 us (60%)
  blocking collectives  302 us (17%)
  other arithmetic  155 us (9%)
  matrix products  122 us (7%)
  local copies, waits for them, and re-layouts  75.7 us (4%)
  between operations  17.6 us (1%)
    reduce_scatter x1, waiting for transfers between devices, local(): lax.psum_scatter(partial_rows.astype(jnp.bfloat16), 'grp', scatter_dimens...  408 us
    all_gather x1, waiting for transfers between devices, local(): lax.all_gather(table_w.astype(jnp.bfloat16), 'grp', axis=0, tiled=True)  357 us
    reduce_scatter x1, waiting for transfers between devices, local(): lax.psum_scatter(grad_ffn, ('grp', 'row'), scatter_dimension=0, tiled=True)  134 us
    reduce_scatter x1, waiting for transfers between devices, local(): lax.psum_scatter(grad_attn, ('grp', 'row'), scatter_dimension=0, tiled=True)  131 us
    psum x1, blocking collectives, local(): valid_total = lax.psum(jnp.sum(flags).astype(jnp.float32), ('grp', 'row'))  74.9 us
    all_gather x1, blocking collectives, local(): lax.all_gather(corr_own, ('grp', 'row'), axis=0, tiled=True)  49 us
    all_gather x1, blocking collectives, local(): lax.all_gather(small_w.astype(jnp.bfloat16), ('grp', 'row'), axis=0, tile...  42.7 us
    all_gather x1, blocking collectives, local(): lax.all_gather(attn_w.astype(jnp.bfloat16), ('grp', 'row'), axis=0, tiled...  39.6 us
  transfers between devices with their start and end apart: 10, of which 7 were waited for; matrix products, arithmetic and copies ran while one was open for 16% of the time, Pallas kernels for 0%

commit v1 on v0

v1 whole, which is shorter than its diff:
```python
import functools
import math

import jax
import jax.numpy as jnp
from jax import lax
from jax.experimental import pallas as pl
from jax.experimental.pallas import tpu as pltpu
from jax.sharding import PartitionSpec as P

D = 256
HEADS = 8
HEAD = 32
FF = 1024
QKV = 3 * D
ATTN = 4 * D
DOWN = ATTN + FF
TABLES = ATTN + 2 * FF
NSMALL = 11
SMALL = 128
META = 16

norm_eps = 1e-05
score_scale = 0.125
logit_scale = 0.125
momentum_rate = 0.5
average_rate = 0.5
negative = -1e30
bf16 = jnp.bfloat16
f32 = jnp.float32
i32 = jnp.int32


def iota(shape, dim, dtype=i32):
    return lax.broadcasted_iota(i32, shape, dim).astype(dtype)


def hot(condition):
    return jnp.where(condition, 1.0, 0.0).astype(bf16)


def dot(left, right):
    return lax.dot_general(left, right, (((1,), (0,)), ((), ())), preferred_element_type=f32)


def dot_cols(left, right):
    return lax.dot_general(left, right, (((1,), (1,)), ((), ())), preferred_element_type=f32)


def split(value):
    high = value.astype(bf16)
    rest = value - high.astype(f32)
    middle = rest.astype(bf16)
    low = (rest - middle.astype(f32)).astype(bf16)
    return (high, middle, low)


def run(body, outs, args, smem=(), scratch=(), flops=0, moved=0, vmem=56):
    return pl.pallas_call(
        body,
        out_shape=[jax.ShapeDtypeStruct(shape, dtype) for shape, dtype in outs],
        in_specs=[
            pl.BlockSpec(memory_space=pltpu.SMEM if i in smem else pltpu.VMEM)
            for i in range(len(args))
        ],
        out_specs=[pl.BlockSpec(memory_space=pltpu.VMEM) for unused in outs],
        scratch_shapes=list(scratch),
        compiler_params=pltpu.CompilerParams(vmem_limit_bytes=vmem << 20),
        cost_estimate=pl.CostEstimate(flops=flops, bytes_accessed=moved, transcendentals=0),
    )(*args)


def route_kernel(cap, dest_ref, local_ref, valid_ref, wanted_ref, place_ref, column_ref, rank_ref):
    devices, width = wanted_ref.shape
    asks = dest_ref.shape[1]
    dest = dest_ref[...]
    local = local_ref[...]
    named = jnp.where(iota((devices, asks), 0) == dest, 1.0, 0.0)
    earlier = hot(iota((asks, asks), 0) < iota((asks, asks), 1))
    before = dot(named.astype(bf16), earlier)
    rank = jnp.sum(named * before, axis=0, keepdims=True)
    count = jnp.sum(named, axis=1, keepdims=True)
    spot = iota((width, asks), 0, f32)
    at_spot = hot((spot == rank) & (spot < cap))
    high = (local >> 6).astype(f32)
    low = (local & 63).astype(f32)
    ids = dot_cols((named * high).astype(bf16), at_spot) * 64.0 + dot_cols(
        (named * low).astype(bf16), at_spot
    )
    lane = iota((devices, width), 1, f32)
    most = jnp.max(count, axis=0, keepdims=True)
    flags = jnp.sum(valid_ref[...].astype(f32), axis=1, keepdims=True)
    ids = jnp.where(lane < jnp.minimum(count, cap), ids, -1.0)
    ids = jnp.where(lane == cap, count, ids)
    ids = jnp.where(lane == cap + 1, most, ids)
    ids = jnp.where(lane == cap + 2, flags, ids)
    wanted_ref[...] = ids.astype(i32)
    place = jnp.where(rank < cap, dest.astype(f32) * cap + rank, -1.0)
    place_ref[...] = place.astype(i32)
    rank_ref[...] = rank.astype(i32)
    column_ref[...] = jnp.broadcast_to(place, (128, asks)).T[:, :1].astype(i32)


def lookup_kernel(cap, asked_ref, table_ref, rows_ref, held):
    devices = asked_ref.shape[0]
    step = 512

    def clear(i, carry):
        held[pl.ds(pl.multiple_of(i * step, step), step), :] = jnp.zeros((step, D), f32)
        return carry

    lax.fori_loop(0, held.shape[0] // step, clear, 0)

    def one_device(n, carry):
        count = jnp.minimum(asked_ref[n, cap], cap)

        def eight(k, carry):
            for j in range(8):
                row = jnp.maximum(asked_ref[n, k * 8 + j], 0)
                held[pl.ds(n * cap + k * 8 + j, 1), :] = table_ref[pl.ds(row, 1), :]
            return carry

        lax.fori_loop(0, (count + 7) // 8, eight, 0)
        return carry

    lax.fori_loop(0, devices, one_device, 0)

    def low(i, carry):
        part = pl.ds(pl.multiple_of(i * step, step), step)
        rows_ref[part, :] = held[part, :].astype(bf16)
        return carry

    lax.fori_loop(0, held.shape[0] // step, low, 0)


def extract_kernel(found_ref, column_ref, freq_ref, logfreq_ref, item_ref, target_ref):
    slots = item_ref.shape[0]
    queries = freq_ref.shape[1]
    block = 256
    total = found_ref.shape[0]

    def rows_of(begin):
        place = column_ref[pl.ds(begin, block), :]
        return dot(hot(place == iota((block, total), 1)), found_ref[...]).astype(bf16)

    def items(i, carry):
        begin = pl.multiple_of(i * block, block)
        item_ref[pl.ds(begin, block), :] = rows_of(begin)
        return carry

    lax.fori_loop(0, slots // block, items, 0)
    target_ref[:queries, :] = rows_of(slots)
    entries = logfreq_ref.shape[1]
    corr = dot(logfreq_ref[...], hot(iota((entries, queries), 0) == freq_ref[...]))
    target_ref[queries:, :] = jnp.broadcast_to(corr, (META, queries)).astype(bf16)


def centred(values):
    centre = values - jnp.mean(values, axis=-1, keepdims=True)
    spread = jnp.mean(centre * centre, axis=-1, keepdims=True)
    scale = lax.rsqrt(spread + norm_eps)
    return (centre * scale, scale)


def norm_back(grad, unit, scale, gain):
    inner = grad * gain
    grad_in = scale * (
        inner
        - jnp.mean(inner, axis=-1, keepdims=True)
        - unit * jnp.mean(inner * unit, axis=-1, keepdims=True)
    )
    return (
        grad_in,
        jnp.sum(grad * unit, axis=0, keepdims=True),
        jnp.sum(grad, axis=0, keepdims=True),
    )


def places_of(seg):
    slots = seg.shape[0]
    lane = iota((slots, 128), 1)
    below = jnp.sum(jnp.where(seg < lane, 1.0, 0.0), axis=0, keepdims=True)
    start = jnp.sum(jnp.where(seg == lane, below, 0.0), axis=1, keepdims=True)
    return iota((slots, 1), 0) - start.astype(i32)


def small_rows(dense_ref, begin):
    return dense_ref[:, begin:].astype(f32).T


def mask_bias(seg, slots_q):
    shape = (seg.shape[0], slots_q.shape[1])
    slot = iota(shape, 0)
    wide = seg.astype(f32)
    seg_q = jnp.sum(jnp.where(slot == slots_q, wide, 0.0), axis=0, keepdims=True)
    return jnp.where((wide == seg_q) & (slot <= slots_q), 0.0, negative)


def forward_kernel(
    item_ref,
    seg_ref,
    slot_row_ref,
    slot_col_ref,
    dense_ref,
    query_ref,
    first_ref,
    normed_ref,
    kv_ref,
    q_ref,
    mixed_ref,
    lse_ref,
    second_ref,
    normed_b_ref,
    active_ref,
    third_ref,
    bias_ref,
    value_t_ref,
    mixed_t_ref,
):
    slots = item_ref.shape[0]
    queries = slot_row_ref.shape[1]
    small_at = dense_ref.shape[1] - SMALL
    pos = dense_ref[:, TABLES:small_at]
    rows = small_rows(dense_ref, small_at)
    seg = seg_ref[...]
    pos_hot = hot(places_of(seg) == iota((slots, small_at - TABLES), 1))
    first = item_ref[...].astype(f32) + dot_cols(pos_hot, pos)
    first_ref[...] = first
    unit, unused = centred(first)
    normed = (unit * rows[0:1] + rows[1:2]).astype(bf16)
    normed_ref[...] = normed
    kv_ref[...] = dot(normed, dense_ref[:, D:QKV]).astype(bf16)
    choose = hot(slot_col_ref[...] == iota((queries, slots), 1))
    normed_q = dot(choose, normed).astype(bf16)
    q_ref[...] = dot(normed_q, dense_ref[:, :D]).astype(bf16)
    first_q = dot(choose, item_ref[...]) + dot_cols(dot(choose, pos_hot).astype(bf16), pos)
    bias_ref[...] = mask_bias(seg, slot_row_ref[...])
    value_t_ref[...] = kv_ref[:, D:].T

    def one_head(h, carry):
        own = iota((1, D), 1) // HEAD == h
        q_own = jnp.where(own, q_ref[...].astype(f32) * score_scale, 0.0).astype(bf16)
        scores = dot_cols(kv_ref[:, :D], q_own) + bias_ref[...]
        top = jnp.max(scores, axis=0, keepdims=True)
        weight = jnp.exp(scores - top)
        total = jnp.sum(weight, axis=0, keepdims=True)
        lse_ref[pl.ds(h, 1), :] = top + jnp.log(total)
        part = pl.ds(pl.multiple_of(h * HEAD, HEAD), HEAD)
        mixed_t_ref[part, :] = dot(value_t_ref[part, :], (weight * (1.0 / total)).astype(bf16))
        return carry

    lax.fori_loop(0, HEADS, one_head, 0)
    mixed = mixed_t_ref[...].T.astype(bf16)
    mixed_ref[...] = mixed
    second = first_q + dot(mixed, dense_ref[:, QKV:ATTN])
    second_ref[...] = second
    unit, unused = centred(second)
    normed_b = (unit * rows[2:3] + rows[3:4]).astype(bf16)
    normed_b_ref[...] = normed_b
    up_bias = jnp.concatenate([rows[7 + k : 8 + k] for k in range(FF // D)], axis=1)
    hidden = dot(normed_b, dense_ref[:, ATTN:DOWN]) + up_bias
    active = jnp.maximum(hidden, 0.0).astype(bf16)
    active_ref[...] = active
    third = second + dot_cols(active, dense_ref[:, DOWN:TABLES]) + rows[6:7]
    third_ref[...] = third
    unit, unused = centred(third)
    query_ref[...] = (unit * rows[4:5] + rows[5:6]).astype(bf16)


def totals_kernel(query_ref, target_ref, out_ref, target_t_ref, corr_ref):
    owners, height, unused = out_ref.shape
    queries = query_ref.shape[0] // owners
    grps = target_ref.shape[0]
    corr_rows = jnp.concatenate(
        [target_ref[g, queries : queries + 1, :].astype(f32) for g in range(grps)]
        + [jnp.zeros((128 - grps, queries), f32)],
        axis=0,
    )
    corr_ref[...] = corr_rows.T

    for g in range(grps):
        target_t_ref[:, g * queries : (g + 1) * queries] = target_ref[g, :queries, :].T

    def one_owner(r, carry):
        begin = pl.multiple_of(r * queries, queries)
        query = (query_ref[pl.ds(begin, queries), :].astype(f32) * logit_scale).astype(bf16)
        logits = [
            dot_cols(target_ref[g, :queries, :], query) - corr_ref[:, g : g + 1]
            for g in range(grps)
        ]
        top = functools.reduce(jnp.maximum, [jnp.max(x, axis=0, keepdims=True) for x in logits])
        total = jnp.zeros((1, queries), f32)
        mixed = jnp.zeros((D, queries), f32)
        for g in range(grps):
            weight = jnp.exp(logits[g] - top)
            total = total + jnp.sum(weight, axis=0, keepdims=True)
            mixed = mixed + dot(
                target_t_ref[:, g * queries : (g + 1) * queries], weight.astype(bf16)
            )
        out_ref[r, :D, :] = mixed.astype(bf16)
        pieces = split(top) + split(total)
        fill = jnp.zeros((META - len(pieces), queries), f32)
        out_ref[r, D:, :] = jnp.concatenate(
            [x.astype(f32) for x in pieces] + [fill], axis=0
        ).astype(bf16)
        return carry

    lax.fori_loop(0, owners, one_owner, 0)


def backward_kernel(
    parts_ref,
    target_ref,
    valid_ref,
    total_ref,
    seg_ref,
    slot_row_ref,
    slot_col_ref,
    dense_ref,
    query_ref,
    first_ref,
    normed_ref,
    kv_ref,
    q_ref,
    mixed_ref,
    lse_ref,
    second_ref,
    normed_b_ref,
    active_ref,
    third_ref,
    grad_first_ref,
    grads_ref,
    sums_ref,
    bias_ref,
    key_t_ref,
    grad_q_t_ref,
    grad_o_ref,
    probs_ref,
    grad_s_ref,
    stack_ref,
    p_ref,
    dp_ref,
):
    owners = parts_ref.shape[0]
    queries = slot_row_ref.shape[1]
    slots = seg_ref.shape[0]
    small_at = dense_ref.shape[1] - SMALL
    rows = small_rows(dense_ref, small_at)
    seg = seg_ref[...]

    tops, totals = [], []
    for r in range(owners):
        tail = parts_ref[r, D:, :].astype(f32)
        tops.append(tail[0:1] + tail[1:2] + tail[2:3])
        totals.append(tail[3:4] + tail[4:5] + tail[5:6])
    top = functools.reduce(jnp.maximum, tops)
    scales = [jnp.exp(x - top) for x in tops]
    total = sum(x * y for x, y in zip(scales, totals))
    log_total = top + jnp.log(total)
    weight = valid_ref[...].astype(f32) / total_ref[0, 0]
    mean_t = jnp.zeros((D, queries), f32)
    for r in range(owners):
        mean_t = mean_t + parts_ref[r, :D, :].astype(f32) * (scales[r] / total)
    target = target_ref[:queries, :].astype(f32)
    grad_query = ((mean_t - target.T) * (weight * logit_scale)).T
    own = jnp.sum((query_ref[...].astype(f32) * target).T, axis=0, keepdims=True) * logit_scale
    own = own - target_ref[queries : queries + 1, :].astype(f32)
    loss = jnp.sum(weight * (log_total - own), axis=1, keepdims=True)
    sums_ref[...] = jnp.concatenate(
        [log_total, weight, jnp.broadcast_to(loss, (1, queries)), jnp.zeros((5, queries), f32)],
        axis=0,
    )

    unit, scale = centred(third_ref[...])
    grad_third, gain_f, shift_f = norm_back(grad_query, unit, scale, rows[4:5])
    grad_f = grad_third.astype(bf16)
    active = active_ref[...]
    grads_ref[:, DOWN:TABLES] = dot(grad_f.T, active).astype(bf16)
    down_bias = jnp.sum(grad_f.astype(f32), axis=0, keepdims=True)
    grad_active = dot(grad_f, dense_ref[:, DOWN:TABLES])
    grad_hidden = jnp.where(active.astype(f32) > 0.0, grad_active, 0.0).astype(bf16)
    grads_ref[:, ATTN:DOWN] = dot(normed_b_ref[...].T, grad_hidden).astype(bf16)
    up_bias = jnp.sum(grad_hidden.astype(f32), axis=0, keepdims=True)
    grad_b = dot_cols(grad_hidden, dense_ref[:, ATTN:DOWN])
    unit, scale = centred(second_ref[...])
    through, gain_b, shift_b = norm_back(grad_b, unit, scale, rows[2:3])
    grad_second = grad_third + through
    grad_y = grad_second.astype(bf16)
    grads_ref[:, QKV:ATTN] = dot(mixed_ref[...].T, grad_y).astype(bf16)
    grad_o_ref[...] = dot_cols(grad_y, dense_ref[:, QKV:ATTN]).astype(bf16)

    bias_ref[...] = mask_bias(seg, slot_row_ref[...])
    key_t_ref[...] = kv_ref[:, :D].T

    def one_head(h, carry):
        own = iota((1, D), 1) // HEAD == h
        q_own = jnp.where(own, q_ref[...].astype(f32), 0.0)
        stack_ref[0, pl.ds(pl.multiple_of(h * queries, queries), queries), :] = q_own.astype(bf16)
        o_own = jnp.where(own, grad_o_ref[...].astype(f32), 0.0).astype(bf16)
        stack_ref[1, pl.ds(pl.multiple_of(h * queries, queries), queries), :] = o_own
        scores = dot_cols(kv_ref[:, :D], (q_own * score_scale).astype(bf16)) + bias_ref[...]
        probs = jnp.exp(scores - lse_ref[pl.ds(h, 1), :])
        p_ref[...] = probs
        columns = pl.ds(pl.multiple_of(h * queries, queries), queries)
        probs_ref[:, columns] = probs.astype(bf16)
        grad_p = dot_cols(kv_ref[:, D:], o_own)
        dp_ref[...] = grad_p
        inner = jnp.sum(p_ref[...] * grad_p, axis=0, keepdims=True)
        grad_s = (p_ref[...] * (dp_ref[...] - inner)).astype(bf16)
        grad_s_ref[:, columns] = grad_s
        part = pl.ds(pl.multiple_of(h * HEAD, HEAD), HEAD)
        grad_q_t_ref[part, :] = dot(key_t_ref[part, :], grad_s)
        return carry

    lax.fori_loop(0, HEADS, one_head, 0)
    grad_q = (grad_q_t_ref[...].T * score_scale).astype(bf16)
    grad_k = (dot(grad_s_ref[...], stack_ref[0]) * score_scale).astype(bf16)
    grad_v = dot(probs_ref[...], stack_ref[1]).astype(bf16)
    normed = normed_ref[...]
    normed_t = normed.T
    grads_ref[:, D : 2 * D] = dot(normed_t, grad_k).astype(bf16)
    grads_ref[:, 2 * D : QKV] = dot(normed_t, grad_v).astype(bf16)
    spread = hot(iota((slots, queries), 0) == slot_row_ref[...])
    grad_q_all = dot(spread, grad_q).astype(bf16)
    grads_ref[:, :D] = dot(normed_t, grad_q_all).astype(bf16)
    grad_a = (
        dot_cols(grad_q_all, dense_ref[:, :D])
        + dot_cols(grad_k, dense_ref[:, D : 2 * D])
        + dot_cols(grad_v, dense_ref[:, 2 * D : QKV])
    )
    unit, scale = centred(first_ref[...])
    through, gain_a, shift_a = norm_back(grad_a, unit, scale, rows[0:1])
    high, middle, low = split(grad_second)
    grad_first = through + ((dot(spread, high) + dot(spread, middle)) + dot(spread, low))
    grad_first_ref[...] = grad_first.astype(bf16)
    pos_hot = hot(places_of(seg) == iota((slots, small_at - TABLES), 1))
    high, middle, low = split(grad_first)
    grads_ref[:, TABLES:small_at] = (dot(high.T, pos_hot) + dot(middle.T, pos_hot)).astype(bf16)
    columns = jnp.concatenate(
        [gain_a, shift_a, gain_b, shift_b, gain_f, shift_f, down_bias]
        + [up_bias[:, k * D : (k + 1) * D] for k in range(FF // D)]
        + [jnp.zeros((SMALL - NSMALL, D), f32)],
        axis=0,
    )
    grads_ref[:, small_at:] = columns.T.astype(bf16)


def target_grad_kernel(
    owners, where_ref, query_ref, target_ref, sums_ref, out_ref, corr_ref
):
    grps = target_ref.shape[0]
    queries = query_ref.shape[0] // owners
    corr_rows = jnp.concatenate(
        [target_ref[g, queries : queries + 1, :].astype(f32) for g in range(grps)]
        + [jnp.zeros((128 - grps, queries), f32)],
        axis=0,
    )
    corr_ref[...] = corr_rows.T
    same = jnp.where(iota((queries, queries), 0) == iota((queries, queries), 1), 1.0, 0.0)
    own_g, own_r = where_ref[0, 0], where_ref[0, 1]
    loss = functools.reduce(jnp.add, [sums_ref[8 * r + 2 : 8 * r + 3, :] for r in range(owners)])
    pieces = split(loss)
    tail = jnp.concatenate(
        [x.astype(f32) for x in pieces] + [jnp.zeros((META - len(pieces), queries), f32)], axis=0
    ).astype(bf16)
    for g in range(grps):
        target = target_ref[g, :queries, :]
        grad = jnp.zeros((queries, D), f32)
        for r in range(owners):
            query = query_ref[r * queries : (r + 1) * queries, :]
            logits = dot_cols(target, query) * logit_scale - corr_ref[:, g : g + 1]
            hit = jnp.where((own_g == g) & (own_r == r), 1.0, 0.0)
            coeff = sums_ref[8 * r + 1 : 8 * r + 2, :] * (
                jnp.exp(logits - sums_ref[8 * r : 8 * r + 1, :]) - hit * same
            )
            grad = grad + dot(coeff.astype(bf16), query)
        out_ref[g, :queries, :] = grad.astype(bf16)
        out_ref[g, queries:, :] = tail


def send_kernel(grad_first_ref, parts_ref, place_ref, sent_ref, both_ref):
    grps, height, unused = parts_ref.shape
    slots = grad_first_ref.shape[0]
    queries = height - META
    both_ref[:slots, :] = grad_first_ref[...]
    total = parts_ref[0, :queries, :].astype(f32)
    for g in range(1, grps):
        total = total + parts_ref[g, :queries, :].astype(f32)
    both_ref[slots:, :] = (total * logit_scale).astype(bf16)
    block = 256
    asks = both_ref.shape[0]

    def one_block(i, carry):
        begin = pl.multiple_of(i * block, block)
        spread = hot(place_ref[...] - begin == iota((block, asks), 0))
        sent_ref[pl.ds(begin, block), :] = dot(spread, both_ref[...]).astype(bf16)
        return carry

    lax.fori_loop(0, sent_ref.shape[0] // block, one_block, 0)


def advance(weight, moment, average, grad, rate):
    moment_new = momentum_rate * moment + grad
    weight_new = weight - rate * (grad + momentum_rate * moment_new)
    average_new = average_rate * average + (1.0 - average_rate) * weight_new
    return (weight_new, moment_new, average_new, weight_new.astype(bf16))


def update_kernel(
    rate, ids_ref, recv_ref, w_ref, m_ref, a_ref, w_out_ref, m_out_ref, a_out_ref, copy_ref
):
    rows = w_ref.shape[0]
    base = pl.program_id(0) * rows
    spread = hot(ids_ref[...] - base == iota((rows, ids_ref.shape[1]), 0))
    grad = dot(spread, recv_ref[...])
    new = advance(w_ref[...], m_ref[...], a_ref[...], grad, rate)
    w_out_ref[...], m_out_ref[...], a_out_ref[...], copy_ref[...] = new


def update_table(ids, recv, table_w, table_m, table_a, rate):
    rows = 368
    count = table_w.shape[0]
    block = pl.BlockSpec((rows, D), lambda i: (i, 0))
    whole = [pl.BlockSpec(memory_space=pltpu.VMEM)] * 2
    return tuple(
        pl.pallas_call(
            functools.partial(update_kernel, rate),
            grid=(pl.cdiv(count, rows),),
            in_specs=whole + [block] * 3,
            out_specs=[block] * 4,
            out_shape=[jax.ShapeDtypeStruct((count, D), f32)] * 3
            + [jax.ShapeDtypeStruct((count, D), bf16)],
            compiler_params=pltpu.CompilerParams(vmem_limit_bytes=56 << 20),
            cost_estimate=pl.CostEstimate(
                flops=2 * count * recv.shape[0] * D, bytes_accessed=26 * count * D, transcendentals=0
            ),
        )(ids, recv, table_w, table_m, table_a)
    )


def everyone(values):
    return lax.all_to_all(values, ("grp", "row"), split_axis=0, concat_axis=0, tiled=True)


def local(
    item_owner,
    item_row,
    seg,
    query_slot,
    tgt_owner,
    tgt_row,
    freq_idx,
    valid,
    logfreq,
    table_w,
    table_m,
    table_a,
    attn_w,
    attn_m,
    attn_a,
    ffn_w,
    ffn_m,
    ffn_a,
    pos_w,
    pos_m,
    pos_a,
    small_w,
    small_m,
    small_a,
):
    owners = lax.axis_size("row")
    grps = lax.axis_size("grp")
    devices = grps * owners
    local_rows = table_w.shape[0]
    slots = seg.shape[1]
    queries = query_slot.shape[1]
    asks = slots + queries
    total_q = queries * devices
    mean = 2 * asks // devices
    cap = 16 * math.ceil((mean + 3.5 * math.sqrt(mean)) / 16)
    width = 128 * math.ceil((cap + 3) / 128)
    maxlen = pos_w.shape[1]
    own_rows = attn_w.shape[0]
    my_grp, my_row = lax.axis_index("grp"), lax.axis_index("row")

    dense = lax.all_gather(
        jnp.concatenate(
            [
                attn_w.astype(bf16),
                ffn_w.astype(bf16),
                pos_w.astype(bf16),
                jnp.pad(small_w.astype(bf16), ((0, 0), (0, SMALL - NSMALL))),
            ],
            axis=1,
        ),
        ("grp", "row"),
        axis=0,
        tiled=True,
    )

    owner_all = jnp.concatenate(
        [item_owner.reshape(1, slots), tgt_owner.reshape(1, queries)], axis=1
    )
    row_all = jnp.concatenate([item_row, tgt_row], axis=1)
    part = row_all // local_rows
    local_row = row_all - part * local_rows
    dest = part * owners + owner_all
    wanted, place, place_col, rank = run(
        functools.partial(route_kernel, cap),
        [((devices, width), i32), ((1, asks), i32), ((asks, 1), i32), ((1, asks), i32)],
        [dest, local_row, valid],
        flops=2 * devices * asks * asks,
    )
    asked = everyone(wanted)
    most = jnp.max(asked[:, cap + 1])
    rounds = (most + cap - 1) // cap
    valid_total = jnp.maximum(jnp.sum(asked[:, cap + 2]).astype(f32), 1.0).reshape(1, 1)
    (rows_found,) = run(
        functools.partial(lookup_kernel, cap),
        [((devices * cap, D), bf16)],
        [asked, table_w],
        smem=(0,),
        scratch=[pltpu.VMEM((devices * cap, D), f32)],
        moved=8 * local_rows * D,
    )
    found = everyone(rows_found.reshape(devices, cap, D)).reshape(devices * cap, D)
    item_emb, target_emb = run(
        extract_kernel,
        [((slots, D), bf16), ((queries + META, D), bf16)],
        [found, place_col, freq_idx, logfreq.reshape(1, -1)],
        flops=2 * devices * cap * asks * D,
    )

    def wanted_of(k):
        here = rank[0] // cap == k
        spot = jnp.where(here, dest[0] * cap + rank[0] - k * cap, devices * cap)
        ids = jnp.full((devices * cap,), -1, i32).at[spot].set(local_row[0], mode="drop")
        return here, spot, everyone(ids.reshape(devices, cap)).reshape(devices * cap)

    def more_rows(both):
        def one_round(carry):
            k, items, targets = carry
            here, spot, ids = wanted_of(k)
            rows = jnp.where((ids >= 0)[:, None], table_w[jnp.maximum(ids, 0)], 0.0).astype(bf16)
            got = everyone(rows.reshape(devices, cap, D)).reshape(devices * cap, D)
            got = got[jnp.minimum(spot, devices * cap - 1)]
            items = jnp.where(here[:slots, None], got[:slots], items)
            top = jnp.where(here[slots:, None], got[slots:], targets[:queries])
            return (k + 1, items, targets.at[:queries].set(top))

        return lax.while_loop(lambda c: c[0] < rounds, one_round, (jnp.int32(1),) + both)[1:]

    item_emb, target_emb = lax.cond(
        rounds > 1, more_rows, lambda both: both, (item_emb, target_emb)
    )

    targets = lax.all_to_all(
        jnp.broadcast_to(target_emb[None], (grps, queries + META, D)),
        "grp",
        split_axis=0,
        concat_axis=0,
        tiled=True,
    )
    seg_col = seg.reshape(slots, 1)
    slot_col = query_slot.reshape(queries, 1)
    query_own, *kept = run(
        forward_kernel,
        [
            ((queries, D), bf16),
            ((slots, D), f32),
            ((slots, D), bf16),
            ((slots, 2 * D), bf16),
            ((queries, D), bf16),
            ((queries, D), bf16),
            ((HEADS, queries), f32),
            ((queries, D), f32),
            ((queries, D), bf16),
            ((queries, FF), bf16),
            ((queries, D), f32),
        ],
        [item_emb, seg_col, query_slot, slot_col, dense],
        scratch=[
            pltpu.VMEM((slots, queries), f32),
            pltpu.VMEM((D, slots), bf16),
            pltpu.VMEM((D, queries), f32),
        ],
        flops=6 << 30,
    )
    query_all = lax.all_gather(query_own, "row", axis=0, tiled=True)
    (mixed,) = run(
        totals_kernel,
        [((owners, D + META, queries), bf16)],
        [query_all, targets],
        scratch=[pltpu.VMEM((D, grps * queries), bf16), pltpu.VMEM((queries, 128), f32)],
        flops=4 * owners * grps * queries * queries * D,
    )
    mixed = lax.all_to_all(mixed, "row", split_axis=0, concat_axis=0, tiled=True)
    grad_first, grads, sums = run(
        backward_kernel,
        [((slots, D), bf16), ((D, dense.shape[1]), bf16), ((8, queries), f32)],
        [mixed, target_emb, valid, valid_total, seg_col, query_slot, slot_col, dense, query_own]
        + kept,
        smem=(3,),
        scratch=[
            pltpu.VMEM((slots, queries), f32),
            pltpu.VMEM((D, slots), bf16),
            pltpu.VMEM((D, queries), f32),
            pltpu.VMEM((queries, D), bf16),
            pltpu.VMEM((slots, HEADS * queries), bf16),
            pltpu.VMEM((slots, HEADS * queries), bf16),
            pltpu.VMEM((2, HEADS * queries, D), bf16),
            pltpu.VMEM((slots, queries), f32),
            pltpu.VMEM((slots, queries), f32),
        ],
        flops=12 << 30,
    )
    sums_all = lax.all_gather(sums, "row", axis=0, tiled=True)
    (target_parts,) = run(
        functools.partial(target_grad_kernel, owners),
        [((grps, queries + META, D), bf16)],
        [jnp.stack([my_grp, my_row]).astype(i32).reshape(1, 2), query_all, targets, sums_all],
        smem=(0,),
        scratch=[pltpu.VMEM((queries, 128), f32)],
        flops=4 * owners * grps * queries * queries * D,
    )
    target_parts = lax.all_to_all(target_parts, "grp", split_axis=0, concat_axis=0, tiled=True)
    loss = jnp.sum(target_parts[:, queries : queries + 3, 0].astype(f32))

    sent, both = run(
        send_kernel,
        [((devices * cap, D), bf16), ((asks, D), bf16)],
        [grad_first, target_parts, place],
        flops=2 * devices * cap * asks * D,
    )
    received = everyone(sent.reshape(devices, cap, D)).reshape(devices * cap, D)

    held = grads.reshape(grps, owners, own_rows, -1)
    bit = 1
    while bit < owners:
        pairs = held.reshape(grps, held.shape[1] // 2, 2, own_rows, -1)
        mine = (my_row // bit) % 2
        keep = lax.dynamic_index_in_dim(pairs, mine, 2, keepdims=False)
        give = lax.dynamic_index_in_dim(pairs, 1 - mine, 2, keepdims=False)
        got = lax.ppermute(give, "row", [(i, i ^ bit) for i in range(owners)])
        held = (keep.astype(f32) + got.astype(f32)).astype(bf16)
        bit *= 2
    held = lax.all_to_all(
        held.reshape(grps, own_rows, -1), "grp", split_axis=0, concat_axis=0, tiled=True
    )
    grad_own = jnp.sum(held.astype(f32), axis=0)

    rate_table = 4.0 * total_q
    rate_dense = 0.25 * math.sqrt(total_q)
    rate_place = 2.0 * math.sqrt(total_q)
    ids = asked[:, :cap].reshape(1, devices * cap)

    def slow_update(received):
        def add(k, total, ids, rows):
            spot = jnp.where(ids >= 0, ids, local_rows)
            return total.at[spot].add(rows.astype(f32), mode="drop")

        def one_round(carry):
            k, total = carry
            here, spot, more_ids = wanted_of(k)
            rows = jnp.zeros((devices * cap, D), bf16).at[spot].set(both, mode="drop")
            rows = everyone(rows.reshape(devices, cap, D)).reshape(devices * cap, D)
            return (k + 1, add(k, total, more_ids, rows))

        total = add(0, jnp.zeros((local_rows, D), f32), ids[0], received)
        total = lax.while_loop(lambda c: c[0] < rounds, one_round, (jnp.int32(1), total))[1]
        return advance(table_w, table_m, table_a, total, rate_table)

    def fast_update(received):
        return update_table(ids, received, table_w, table_m, table_a, rate_table)

    table_out = lax.cond(rounds > 1, slow_update, fast_update, received)
    place_at = TABLES + maxlen
    return (
        (loss,)
        + table_out
        + advance(attn_w, attn_m, attn_a, grad_own[:, :ATTN], rate_dense)
        + advance(ffn_w, ffn_m, ffn_a, grad_own[:, ATTN:TABLES], rate_dense)
        + advance(pos_w, pos_m, pos_a, grad_own[:, TABLES:place_at], rate_place)
        + advance(
            small_w, small_m, small_a, grad_own[:, place_at : place_at + NSMALL], rate_dense
        )
    )


def solution(mesh):
    rows = P(("grp", "row"), None)
    table = P(("row", "grp"), None)
    ids = P(("grp", "row"), None, None)
    in_specs = (ids, rows, rows, rows, ids, rows, rows, rows, P()) + (table,) * 3 + (rows,) * 12
    out_specs = (P(),) + (table,) * 4 + (rows,) * 16
    return jax.shard_map(local, mesh=mesh, in_specs=in_specs, out_specs=out_specs, check_vma=False)
```

time: 1760 us -> 338 us (0.19)
  waiting for transfers between devices: 1060 us -> 124 us
  blocking collectives: 302 us -> 42.3 us
  other arithmetic: 155 us -> 11.4 us
  matrix products: 122 us -> 0 us
  Pallas kernels: 0 us -> 98.5 us
  local copies, waits for them, and re-layouts: 75.7 us -> 11.3 us
  starting transfers between devices: 8.06 us -> 31.6 us
    reduce_scatter x5 -> x0, waiting for transfers between devices: 687 us -> none  [the longest x1 408 us: local(): lax.psum_scatter(partial_rows.astype(jnp.bfloat16), 'grp', scatter_dimens...]
    all_gather x3 -> x1, waiting for transfers between devices: 372 us -> 5.14 us  [local(): lax.all_gather(jnp.concatenate([attn_w.astype(bf16), ffn_w.astype(bf16),...]
    all_gather x4 -> x2, blocking collectives: 169 us -> 27.9 us  [the longest x1 18.5 us: local(): sums_all = lax.all_gather(sums, 'row', axis=0, tiled=True)]
    dot_general x35 -> x0, matrix products: 122 us -> none  [the longest x4 28.3 us: masked_scores(): jnp.einsum('qhd,khd->hqk', rows_q, heads_k, preferred_element_type=jnp.fl...]
    psum x2 -> x0, blocking collectives: 113 us -> none  [the longest x1 74.9 us: local(): valid_total = lax.psum(jnp.sum(flags).astype(jnp.float32), ('grp', 'row'))]
    all_to_all x2 -> x6, waiting for transfers between devices: 0.01 us -> 108 us  [the longest x2 80.8 us: everyone(): lax.all_to_all(values, ('grp', 'row'), split_axis=0, concat_axis=0, tiled...]
    pallas_call x0 -> x9, Pallas kernels: none -> 98.5 us  [the longest x8 74.2 us: run(): pl.pallas_call(body, out_shape=[jax.ShapeDtypeStruct(shape, dtype) for sh...]
    convert_element_type x20 -> x9, other arithmetic: 65.8 us -> 3.92 us  [the longest x4 2.49 us: advance(): return (weight_new, moment_new, average_new, weight_new.astype(bf16))]
  transfers between devices with their start and end apart: 10 -> 9, of which waited for: 7 -> 7; matrix products, arithmetic and copies ran while one was open for 16% -> 5% of each run, Pallas kernels for 0% -> 10%
where the time goes in v1:
time: 338 us; the launch traced here: 335 us
  waiting for transfers between devices  124 us (37%)
  Pallas kernels  98.5 us (29%)
  blocking collectives  42.3 us (13%)
  starting transfers between devices  31.6 us (9%)
  between operations  15.9 us (5%)
  other arithmetic  11.4 us (3%)
  local copies, waits for them, and re-layouts  11.3 us (3%)
    all_to_all x2, waiting for transfers between devices, everyone(): lax.all_to_all(values, ('grp', 'row'), split_axis=0, concat_axis=0, tiled...  80.8 us
    pallas_call x8, Pallas kernels, run(): pl.pallas_call(body, out_shape=[jax.ShapeDtypeStruct(shape, dtype) for sh...  74.2 us
    pallas_call x1, Pallas kernels, update_table(): pl.pallas_call(functools.partial(update_kernel, rate), grid=(pl.cdiv(coun...  24.3 us
    all_gather x1, blocking collectives, local(): sums_all = lax.all_gather(sums, 'row', axis=0, tiled=True)  18.5 us
    all_to_all x1, blocking collectives, everyone(): lax.all_to_all(values, ('grp', 'row'), split_axis=0, concat_axis=0, tiled...  14.4 us
    all_to_all x1, waiting for transfers between devices, local(): lax.all_to_all(target_parts, 'grp', split_axis=0, concat_axis=0, tiled=True)  12.5 us
    ppermute x2, waiting for transfers between devices, local(): got = lax.ppermute(give, 'row', [(i, i ^ bit) for i in range(owners)])  11.6 us
    all_to_all x2, starting transfers between devices, everyone(): lax.all_to_all(values, ('grp', 'row'), split_axis=0, concat_axis=0, tiled...  10.7 us
  transfers between devices with their start and end apart: 9, of which 7 were waited for; matrix products, arithmetic and copies ran while one was open for 5% of the time, Pallas kernels for 10%

profile of v1, /device:TPU:0, one launch (start us, length us, event | category | flops | bytes accessed | tf_op | source)
XLA Modules:
  0.0 335.4 jit_solution(13309398287031145943)
XLA Ops:
  7.2 0.7 constant_dynamic-update-slice_fusion.1
  7.9 0.7 constant_dynamic-update-slice_fusion
  8.6 0.7 add_add_fusion.dest_ref
  9.3 2.2 shard_map.391
  11.6 14.4 %all_to_all.89 = s32[32,1,128]{2,1,0:T(1,128)S(1)} all-to-all(s32[32,1,128]{2,1,0:T(1,128)} %bitcast.102), channel_id=1, replica_groups=mesh['grp'=8,'row'=4] {'grp','row'}, dimensions={0} | all-to-all | bytes 32768 | tf_op jit(solution)/shard_map/all_to_all | solution.py:542
  25.9 11.9 %shard_map.392 = bf16[3584,256]{1,0:T(8,128)(2,1)} custom-call(s32[32,128]{1,0:T(8,128)S(1)} %bitcast.98, f32[6256,256]{1,0:T(8,128)} %table_ref.1), custom_call_target="tpu_custom_call" | custom-call | bytes 12812288 | tf_op jit(solution)/shard_map/pallas_call | solution.py:59
  37.8 0.0 copy-start.22
  37.8 7.2 %all-to-all-start.5 = ((bf16[32,112,256]{2,1,0:T(8,128)(2,1)}), bf16[32,112,256]{2,1,0:T(8,128)(2,1)S(1)}, u32[]{:S(2)}, u32[]{:S(2)}) async-start(bf16[32,112,256]{2,1,0:T(8,128)(2,1)} %bitcast.89), calls=%async_computation.5 | async-start | bytes 3670016 | tf_op jit(solution)/shard_map/all_to_all | solution.py:542
  45.1 0.0 all-gather.2.cloned.1.call-start
  45.2 0.6 fusion.23
  45.8 0.0 all-gather.2.cloned.1.call-update
  45.9 0.6 reshape.758.logfreq_ref
  46.5 0.7 slice_reduce_fusion
  47.9 44.1 %all-to-all-done.5 = bf16[32,112,256]{2,1,0:T(8,128)(2,1)S(1)} async-done(((bf16[32,112,256]{2,1,0:T(8,128)(2,1)}), bf16[32,112,256]{2,1,0:T(8,128)(2,1)S(1)}, u32[]{:S(2)}, u32[]{:S(2)}) %all-to-all-start.5) | async-done | bytes 1835040 | tf_op jit(solution)/shard_map/all_to_all | solution.py:542
  91.9 1.2 copy-done.2
  93.2 5.2 %shard_map.393 = (bf16[1024,256]{1,0:T(8,128)(2,1)}, bf16[272,256]{1,0:T(8,128)(2,1)S(1)}) custom-call(bf16[3584,256]{1,0:T(8,128)(2,1)} %bitcast.96, s32[1280,1]{1,0:T(8,128)} %get-tuple-element.384.column_ref, s32[1,256]{1,0:T(1,128)} %freq_ref.1, bf16[1,1024]{1,0:T(2,128)(2,1)} %reshape.758.logfreq_ref), custom_call_target="tpu_custom_call" | custom-call | flops 2348810240 | tf_op jit(solution)/shard_map/pallas_call | solution.py:59
  98.4 1.1 broadcast_in_dim.67
  99.5 3.6 %all-to-all-start.6 = ((bf16[8,272,256]{2,1,0:T(8,128)(2,1)}), bf16[8,272,256]{2,1,0:T(8,128)(2,1)S(1)}, u32[]{:S(2)}, u32[]{:S(2)}) async-start(bf16[8,272,256]{2,1,0:T(8,128)(2,1)} %broadcast_in_dim.67), calls=%async_computation.6 | async-start | bytes 2228224 | tf_op jit(solution)/shard_map/all_to_all | solution.py:657
  103.1 1.5 copy.58.slot_col_ref
  104.6 1.7 copy.57.seg_ref
  106.3 5.1 %all-gather.2.cloned.1.call-done.dense_ref = bf16[256,3712]{1,0:T(8,128)(2,1)} async-done(((bf16[8,3712]{1,0:T(8,128)(2,1)}), bf16[256,3712]{1,0:T(8,128)(2,1)}) %all-gather.2.cloned.1.call-update) | async-done | bytes 1900560 | tf_op jit(solution)/shard_map/all_gather | solution.py:586
  111.4 13.8 %shard_map.394 = (bf16[256,256]{1,0:T(8,128)(2,1)}, f32[1024,256]{1,0:T(8,128)}, bf16[1024,256]{1,0:T(8,128)(2,1)}, bf16[1024,512]{1,0:T(8,128)(2,1)}, bf16[256,...) custom-call(bf16[1024,256]{1,0:T(8,128)(2,1)} %get-tuple-element.388, ...), custom_call_target="tpu_custom_call" | custom-call | flops 6442450944 | tf_op jit(solution)/shard_map/pallas_call | solution.py:59
  125.3 9.4 %all_gather.10.query_ref = bf16[1024,256]{1,0:T(8,128)(2,1)} all-gather(bf16[256,256]{1,0:T(8,128)(2,1)} %get-tuple-element.389.query_ref), channel_id=1, replica_groups=mesh['grp'=8,'row'=4] {'row'}, dimensions={0}, use_global_device_ids=true | all-gather | bytes 655360 | tf_op jit(solution)/shard_map/all_gather | solution.py:689
  134.7 0.0 all-to-all-done.6.target_ref
  134.7 1.0 copy-done.3
  135.7 9.4 %shard_map.395 = bf16[4,272,256]{2,1,0:T(8,128)(2,1)} custom-call(bf16[1024,256]{1,0:T(8,128)(2,1)} %all_gather.10.query_ref, bf16[8,272,256]{2,1,0:T(8,128)(2,1)} %copy-done.3), custom_call_target="tpu_custom_call" | custom-call | flops 2147483648 | tf_op jit(solution)/shard_map/pallas_call | solution.py:59
  145.1 3.5 %all-to-all-start.7 = ((bf16[4,272,256]{2,1,0:T(8,128)(2,1)}), bf16[4,272,256]{2,1,0:T(8,128)(2,1)S(1)}, u32[]{:S(2)}, u32[]{:S(2)}) async-start(bf16[4,272,256]{2,1,0:T(8,128)(2,1)} %shard_map.395), calls=%async_computation.7 | async-start | bytes 1114112 | tf_op jit(solution)/shard_map/all_to_all | solution.py:697
  149.2 8.5 %all-to-all-done.7.parts_ref = bf16[4,272,256]{2,1,0:T(8,128)(2,1)S(1)} async-done(((bf16[4,272,256]{2,1,0:T(8,128)(2,1)}), bf16[4,272,256]{2,1,0:T(8,128)(2,1)S(1)}, u32[]{:S(2)}, u32[]{:S(2)}) %all-to-all-start.7) | async-done | bytes 557088 | tf_op jit(solution)/shard_map/all_to_all | solution.py:697
  157.7 0.8 copy-done.4
  158.5 18.6 %shard_map.396 = (bf16[1024,256]{1,0:T(8,128)(2,1)}, bf16[256,3712]{1,0:T(8,128)(2,1)}, f32[8,256]{1,0:T(8,128)}) custom-call(bf16[4,272,256]{2,1,0:T(8,128)(2,1)} %copy-done.4, bf16[272,256]{1,0:T(8,128)(2,1)S(1)} %get-tuple-element.390.target_ref, s32[1,256]{1,0:T(1,128)} %valid_ref.3, f32[1,1]{1,0:T(1,128)} %bitcast.27.total_ref, ...), custom_call_target="tpu_custom_call" | custom-call | flops 12884901888 | tf_op jit(solution)/shard_map/pallas_call | solution.py:59
  177.2 1.3 dynamic-slice_bitcast_fusion
  178.4 0.1 collective-permute-start
  178.6 0.6 add_bitcast_fusion.where_ref
  179.2 18.5 %all_gather.11.sums_ref = f32[32,256]{1,0:T(8,128)} all-gather(f32[8,256]{1,0:T(8,128)} %get-tuple-element.401), channel_id=1, replica_groups=mesh['grp'=8,'row'=4] {'row'}, dimensions={0}, use_global_device_ids=true | all-gather | bytes 40960 | tf_op jit(solution)/shard_map/all_gather | solution.py:717
  197.6 5.4 %shard_map.397 = bf16[8,272,256]{2,1,0:T(8,128)(2,1)} custom-call(s32[1,2]{1,0:T(1,128)} %add_bitcast_fusion.where_ref, bf16[1024,256]{1,0:T(8,128)(2,1)} %all_gather.10.query_ref, bf16[8,272,256]{2,1,0:T(8,128)(2,1)} %copy-done.3, f32[32,256]{1,0:T(8,128)} %all_gather.11.sums_ref), custom_call_target="tpu_custom_call" | custom-call | flops 2147483648 | tf_op jit(solution)/shard_map/pallas_call | solution.py:59
  203.0 8.8 %all-to-all-start.8 = ((bf16[8,272,256]{2,1,0:T(8,128)(2,1)}), bf16[8,272,256]{2,1,0:T(8,128)(2,1)}, u32[]{:S(2)}, u32[]{:S(2)}) async-start(bf16[8,272,256]{2,1,0:T(8,128)(2,1)} %shard_map.397), calls=%async_computation.8 | async-start | bytes 2228224 | tf_op jit(solution)/shard_map/all_to_all | solution.py:726
  211.8 1.4 fusion.20
  213.3 1.3 collective-permute-start.1
  214.6 11.6 %collective-permute-done.1 = bf16[8,1,8,3712]{3,2,1,0:T(8,128)(2,1)S(1)} collective-permute-done((bf16[8,1,8,3712]{3,2,1,0:T(8,128)(2,1)S(1)}, bf16[8,1,8,3712]{3,2,1,0:T(8,128)(2,1)S(1)}, u32[]{:S(2)}, u32[]{:S(2)}) %collective-permute-start.1) | collective-permute-done | bytes 475168 | tf_op jit(solution)/shard_map/ppermute | solution.py:744
  226.2 0.9 fusion.21
  227.1 12.5 %all-to-all-done.8.parts_ref = bf16[8,272,256]{2,1,0:T(8,128)(2,1)} async-done(((bf16[8,272,256]{2,1,0:T(8,128)(2,1)}), bf16[8,272,256]{2,1,0:T(8,128)(2,1)}, u32[]{:S(2)}, u32[]{:S(2)}) %all-to-all-start.8) | async-done | bytes 1114144 | tf_op jit(solution)/shard_map/all_to_all | solution.py:726
  239.5 3.6 %all-to-all-start.10 = ((bf16[8,8,3712]{2,1,0:T(8,128)(2,1)}), bf16[8,8,3712]{2,1,0:T(8,128)(2,1)S(1)}, u32[]{:S(2)}, u32[]{:S(2)}) async-start(bf16[8,8,3712]{2,1,0:T(8,128)(2,1)} %fusion.21), calls=%async_computation.10 | async-start | bytes 950272 | tf_op jit(solution)/shard_map/all_to_all | solution.py:747
  243.2 7.6 %shard_map.398 = (bf16[3584,256]{1,0:T(8,128)(2,1)}, bf16[1280,256]{1,0:T(8,128)(2,1)S(1)}) custom-call(bf16[1024,256]{1,0:T(8,128)(2,1)} %get-tuple-element.402.grad_first_ref, bf16[8,272,256]{2,1,0:T(8,128)(2,1)} %all-to-all-done.8.parts_ref, s32[1,1280]{1,0:T(1,128)} %get-tuple-element.403.place_ref), custom_call_target="tpu_custom_call" | custom-call | flops 2348810240 | tf_op jit(solution)/shard_map/pallas_call | solution.py:59
  250.8 0.0 copy-start.16
  250.8 0.0 copy-start.15
  250.8 0.0 copy-start.14
  250.8 0.0 copy-start.13
  250.9 0.0 copy-start.9
  250.9 5.9 %all-to-all-done.10 = bf16[8,8,3712]{2,1,0:T(8,128)(2,1)S(1)} async-done(((bf16[8,8,3712]{2,1,0:T(8,128)(2,1)}), bf16[8,8,3712]{2,1,0:T(8,128)(2,1)S(1)}, u32[]{:S(2)}, u32[]{:S(2)}) %all-to-all-start.10) | async-done | bytes 475168 | tf_op jit(solution)/shard_map/all_to_all | solution.py:747
  256.8 3.4 %all-to-all-start.9 = ((bf16[32,112,256]{2,1,0:T(8,128)(2,1)}), bf16[32,112,256]{2,1,0:T(8,128)(2,1)S(1)}, u32[]{:S(2)}, u32[]{:S(2)}) async-start(bf16[32,112,256]{2,1,0:T(8,128)(2,1)} %bitcast.97), calls=%async_computation.9 | async-start | bytes 3670016 | tf_op jit(solution)/shard_map/all_to_all | solution.py:542
  260.2 1.3 convert_reduce_fusion.1
  261.6 0.1 convert_reduce_fusion
  261.7 0.6 fusion.26
  262.3 0.6 add_multiply_fusion.4
  262.9 0.6 fusion.27
  263.5 0.6 add_multiply_fusion.3
  264.1 0.6 fusion.29
  264.7 0.6 add_multiply_fusion.2
  265.3 0.7 fusion.28
  266.0 0.6 add_multiply_fusion.1
  266.7 36.7 %all-to-all-done.9 = bf16[32,112,256]{2,1,0:T(8,128)(2,1)S(1)} async-done(((bf16[32,112,256]{2,1,0:T(8,128)(2,1)}), bf16[32,112,256]{2,1,0:T(8,128)(2,1)S(1)}, u32[]{:S(2)}, u32[]{:S(2)}) %all-to-all-start.9) | async-done | bytes 1835040 | tf_op jit(solution)/shard_map/all_to_all | solution.py:542
  303.4 25.0 %conditional.3 = ((f32[6256,256]{1,0:T(8,128)}, f32[6256,256]{1,0:T(8,128)}, f32[6256,256]{1,0:T(8,128)}, bf16[6256,256]{1,0:T(8,128)(2,1)})) conditional(s32[]{:T(128)} %convert_element_type.86, (s32[32,112]{1,0:T(8,128)S(1)}, bf16[3584,256]{1,0:T(8,128)(2,1)S(1)}, f32[6256,256]{1,0:T(8,128)}, f32[6256,256]{1,0:T(8,128)}, ...), branch_computations={%region_8.9_spmd, %region_9.16_spmd} | conditional | flops 11479810048 | bytes 123392464 | solution.py:776
  303.4 0.7 reshape.742.ids_ref
  304.1 24.3 %branch_0_fun.1 = (f32[6256,256]{1,0:T(8,128)}, f32[6256,256]{1,0:T(8,128)}, f32[6256,256]{1,0:T(8,128)}, bf16[6256,256]{1,0:T(8,128)(2,1)}) custom-call(s32[1,3584]{1,0:T(1,128)} %reshape.742.ids_ref, bf16[3584,256]{1,0:T(8,128)(2,1)S(1)} %get-tuple-element.309.recv_ref, f32[6256,256]{1,0:T(8,128)} %get-tuple-element.310.w_ref, ...), custom_call_target="tpu_custom_call" | custom-call | flops 11479810048 | bytes 41639936 | tf_op jit(solution)/shard_map/cond/branch_0_fun/pallas_call | solution.py:526
  (43 shorter events, 0.2 us)
Async XLA Ops:
  37.8 7.3 %copy-start.18 = (f32[8,11]{1,0:T(8,128)S(1)}, f32[8,11]{1,0:T(8,128)}, u32[]{:S(2)}) copy-start(f32[8,11]{1,0:T(8,128)} %param.55) | copy-start | bytes 1060
  37.8 7.3 %copy-start.11 = (f32[8,512]{1,0:T(8,128)S(1)}, f32[8,512]{1,0:T(8,128)}, u32[]{:S(2)}) copy-start(f32[8,512]{1,0:T(8,128)} %param.52) | copy-start | bytes 49156
  37.8 7.4 %copy-start.8 = (f32[8,1024]{1,0:T(8,128)S(1)}, f32[8,1024]{1,0:T(8,128)}, u32[]{:S(2)}) copy-start(f32[8,1024]{1,0:T(8,128)} %param.46) | copy-start | bytes 98308
  37.8 7.4 %copy-start.6 = (f32[8,2048]{1,0:T(8,128)S(1)}, f32[8,2048]{1,0:T(8,128)}, u32[]{:S(2)}) copy-start(f32[8,2048]{1,0:T(8,128)} %param.49) | copy-start | bytes 196612
  37.8 8.1 %copy-start.22 = (bf16[1024]{0:T(1024)(128)(2,1)S(1)}, bf16[1024]{0:T(1024)(128)(2,1)}, u32[]{:S(2)}) copy-start(bf16[1024]{0:T(1024)(128)(2,1)} %param.42) | copy-start | bytes 6148
  37.8 54.1 %all-to-all-start.5 = ((bf16[32,112,256]{2,1,0:T(8,128)(2,1)}), bf16[32,112,256]{2,1,0:T(8,128)(2,1)S(1)}, u32[]{:S(2)}, u32[]{:S(2)}) async-start(bf16[32,112,256]{2,1,0:T(8,128)(2,1)} %bitcast.89), calls=%async_computation.5 | async-start | bytes 3670016 | tf_op jit(solution)/shard_map/all_to_all | solution.py:542
  45.1 66.4 %all-gather.2.cloned.1.call-start = ((), (), s32[]{:S(2)}) async-start(), calls=%async_computation.11 | async-start | bytes 1959936 | tf_op jit(solution)/shard_map/all_gather | solution.py:586
  91.9 1.2 copy-start.2
  99.5 35.2 %all-to-all-start.6 = ((bf16[8,272,256]{2,1,0:T(8,128)(2,1)}), bf16[8,272,256]{2,1,0:T(8,128)(2,1)S(1)}, u32[]{:S(2)}, u32[]{:S(2)}) async-start(bf16[8,272,256]{2,1,0:T(8,128)(2,1)} %broadcast_in_dim.67), calls=%async_computation.6 | async-start | bytes 2228224 | tf_op jit(solution)/shard_map/all_to_all | solution.py:657
  134.7 1.0 copy-start.3
  145.1 12.6 %all-to-all-start.7 = ((bf16[4,272,256]{2,1,0:T(8,128)(2,1)}), bf16[4,272,256]{2,1,0:T(8,128)(2,1)S(1)}, u32[]{:S(2)}, u32[]{:S(2)}) async-start(bf16[4,272,256]{2,1,0:T(8,128)(2,1)} %shard_map.395), calls=%async_computation.7 | async-start | bytes 1114112 | tf_op jit(solution)/shard_map/all_to_all | solution.py:697
  157.7 0.8 copy-start.4
  178.4 33.3 %collective-permute-start = (bf16[8,2,8,3712]{3,2,1,0:T(8,128)(2,1)S(1)}, bf16[8,2,8,3712]{3,2,1,0:T(8,128)(2,1)}, u32[]{:S(2)}, u32[]{:S(2)}) collective-permute-start(bf16[8,2,8,3712]{3,2,1,0:T(8,128)(2,1)S(1)} %dynamic-slice_bitcast_fusion), channel_id=1, source_target_pairs={{0,1},{1,0},{2,3},{3,2},{4,5},{5,4},{6,7},{7,6},{8,9},{9,8},{10,11... | collective-permute-start | bytes 2850824 | tf_op jit(solution)/shard_map/ppermute | solution.py:744
  197.6 14.2 %copy-start.1 = (bf16[256,3712]{1,0:T(8,128)(2,1)S(1)}, bf16[256,3712]{1,0:T(8,128)(2,1)}, u32[]{:S(2)}) copy-start(bf16[256,3712]{1,0:T(8,128)(2,1)} %get-tuple-element.410) | copy-start | bytes 5701636
  203.0 36.5 %all-to-all-start.8 = ((bf16[8,272,256]{2,1,0:T(8,128)(2,1)}), bf16[8,272,256]{2,1,0:T(8,128)(2,1)}, u32[]{:S(2)}, u32[]{:S(2)}) async-start(bf16[8,272,256]{2,1,0:T(8,128)(2,1)} %shard_map.397), calls=%async_computation.8 | async-start | bytes 2228224 | tf_op jit(solution)/shard_map/all_to_all | solution.py:726
  213.3 12.9 %collective-permute-start.1 = (bf16[8,1,8,3712]{3,2,1,0:T(8,128)(2,1)S(1)}, bf16[8,1,8,3712]{3,2,1,0:T(8,128)(2,1)S(1)}, u32[]{:S(2)}, u32[]{:S(2)}) collective-permute-start(bf16[8,1,8,3712]{3,2,1,0:T(8,128)(2,1)S(1)} %constant_dynamic-slice_fusion), channel_id=1, source_target_pairs={{0,2},{1,3},{2,0},{3,1},{4,6},{5,7},{6,4},{7,5},{8,10},{9,11},{10,... | collective-permute-start | bytes 1425416 | tf_op jit(solution)/shard_map/ppermute | solution.py:744
  239.5 17.3 %all-to-all-start.10 = ((bf16[8,8,3712]{2,1,0:T(8,128)(2,1)}), bf16[8,8,3712]{2,1,0:T(8,128)(2,1)S(1)}, u32[]{:S(2)}, u32[]{:S(2)}) async-start(bf16[8,8,3712]{2,1,0:T(8,128)(2,1)} %fusion.21), calls=%async_computation.10 | async-start | bytes 950272 | tf_op jit(solution)/shard_map/all_to_all | solution.py:747
  250.8 10.8 %copy-start.21 = (f32[8,11]{1,0:T(8,128)S(1)}, f32[8,11]{1,0:T(8,128)}, u32[]{:S(2)}) copy-start(f32[8,11]{1,0:T(8,128)} %param.56) | copy-start | bytes 1060
  250.8 11.5 %copy-start.20 = (f32[8,11]{1,0:T(8,128)S(1)}, f32[8,11]{1,0:T(8,128)}, u32[]{:S(2)}) copy-start(f32[8,11]{1,0:T(8,128)} %param.57) | copy-start | bytes 1060
  250.8 12.1 %copy-start.12 = (f32[8,512]{1,0:T(8,128)S(1)}, f32[8,512]{1,0:T(8,128)}, u32[]{:S(2)}) copy-start(f32[8,512]{1,0:T(8,128)} %param.52) | copy-start | bytes 49156
  250.8 12.1 %copy-start.19 = (f32[8,512]{1,0:T(8,128)S(1)}, f32[8,512]{1,0:T(8,128)}, u32[]{:S(2)}) copy-start(f32[8,512]{1,0:T(8,128)} %param.53) | copy-start | bytes 49156
  250.8 12.7 %copy-start.16 = (f32[8,512]{1,0:T(8,128)S(1)}, f32[8,512]{1,0:T(8,128)}, u32[]{:S(2)}) copy-start(f32[8,512]{1,0:T(8,128)} %param.54) | copy-start | bytes 49156
  250.8 13.3 %copy-start.15 = (f32[8,1024]{1,0:T(8,128)S(1)}, f32[8,1024]{1,0:T(8,128)}, u32[]{:S(2)}) copy-start(f32[8,1024]{1,0:T(8,128)} %param.47) | copy-start | bytes 98308
  250.8 13.9 %copy-start.14 = (f32[8,1024]{1,0:T(8,128)S(1)}, f32[8,1024]{1,0:T(8,128)}, u32[]{:S(2)}) copy-start(f32[8,1024]{1,0:T(8,128)} %param.48) | copy-start | bytes 98308
  250.8 14.5 %copy-start.13 = (f32[8,2048]{1,0:T(8,128)S(1)}, f32[8,2048]{1,0:T(8,128)}, u32[]{:S(2)}) copy-start(f32[8,2048]{1,0:T(8,128)} %param.50) | copy-start | bytes 196612
  250.9 15.1 %copy-start.9 = (f32[8,2048]{1,0:T(8,128)S(1)}, f32[8,2048]{1,0:T(8,128)}, u32[]{:S(2)}) copy-start(f32[8,2048]{1,0:T(8,128)} %param.51) | copy-start | bytes 196612
  256.8 46.6 %all-to-all-start.9 = ((bf16[32,112,256]{2,1,0:T(8,128)(2,1)}), bf16[32,112,256]{2,1,0:T(8,128)(2,1)S(1)}, u32[]{:S(2)}, u32[]{:S(2)}) async-start(bf16[32,112,256]{2,1,0:T(8,128)(2,1)} %bitcast.97), calls=%async_computation.9 | async-start | bytes 3670016 | tf_op jit(solution)/shard_map/all_to_all | solution.py:542
  262.3 41.1 %copy-start.17 = (f32[8,11]{1,0:T(8,128)}, f32[8,11]{1,0:T(8,128)S(1)}, u32[]{:S(2)}) copy-start(f32[8,11]{1,0:T(8,128)S(1)} %get-tuple-element.457) | copy-start | bytes 1060
  263.5 39.9 %copy-start.10 = (f32[8,512]{1,0:T(8,128)}, f32[8,512]{1,0:T(8,128)S(1)}, u32[]{:S(2)}) copy-start(f32[8,512]{1,0:T(8,128)S(1)} %get-tuple-element.460) | copy-start | bytes 49156
  264.7 38.7 %copy-start.7 = (f32[8,1024]{1,0:T(8,128)}, f32[8,1024]{1,0:T(8,128)S(1)}, u32[]{:S(2)}) copy-start(f32[8,1024]{1,0:T(8,128)S(1)} %get-tuple-element.466) | copy-start | bytes 98308
  266.0 37.4 %copy-start.5 = (f32[8,2048]{1,0:T(8,128)}, f32[8,2048]{1,0:T(8,128)S(1)}, u32[]{:S(2)}) copy-start(f32[8,2048]{1,0:T(8,128)S(1)} %get-tuple-element.463) | copy-start | bytes 196612
Sparse Core Ops, SparseCore 0:
  49.4 61.9 all-gather.1
